TPU v7x, 128 devices: a whole 4x4x4 slice. The times are simulated.
128 devices in a mesh: grp: 8 (over z, core), ep: 16 (over y, x).
Axes of the slice: x: 4, y: 4, z: 4, core: 2. Of those that a mesh axis runs over, the one named last changes fastest.
Arguments:
- tokens: bfloat16 [16384, 6144], P(('grp', 'ep')), may hold values from -6 to 6
- routed_slots: int32 [7168], P(('grp', 'ep')), may hold values from -1 to 127, as said below
- combine_weight: float32 [7168], P(('grp', 'ep')), may hold values from 0.1 to 1
- gate_weight: bfloat16 [6144, 8192], P('grp', 'ep'), may hold values from -0.078125 to 0.078125
- up_weight: bfloat16 [6144, 8192], P('grp', 'ep'), may hold values from -0.078125 to 0.078125
- down_weight: bfloat16 [8192, 6144], P('ep', 'grp'), may hold values from -0.0625 to 0.0625
Outputs:
- mixed: bfloat16 [16384, 6144], P(('grp', 'ep'))
Inputs may be any that keep to these rules, and one draw needn't show every extreme that they name: `routed_slots`: each owner's 56 slots hold distinct local token numbers, live ones in the first slots and -1 after them; in every draw all 16 owners of one replica have all 56 slots live.
All inputs are finite; a program needn't handle non-finite values.
Results may differ from a plain program's by a relative error of at most 0.019.
Values may be sent and summed in bfloat16 or wider, within the bound.
No kernel may reach another device: no remote copies, remote signals or barrier semaphores. Data moves between devices by JAX's collectives and lax.ppermute only.
A program may use at most 128 MiB of HBM per device.

v0:
```python
import jax
import jax.numpy as jnp
from jax import lax
from jax.sharding import PartitionSpec as P


def on_device(tokens, routed_slots, combine_weight, gate_weight, up_weight, down_weight):
    local_tokens = tokens.shape[0]
    slot_count = routed_slots.shape[0]
    valid = routed_slots >= 0
    safe_slots = jnp.where(valid, routed_slots, 0)
    packed = jnp.where(
        valid[:, None], jnp.take(tokens, safe_slots, axis=0), jnp.zeros((), jnp.bfloat16)
    )
    gathered = lax.all_gather(packed, "ep", axis=0, tiled=True)
    gate_part = jnp.dot(
        gathered,
        lax.all_gather(gate_weight, "grp", axis=0, tiled=True),
        preferred_element_type=jnp.float32,
    )
    up_part = jnp.dot(
        gathered,
        lax.all_gather(up_weight, "grp", axis=0, tiled=True),
        preferred_element_type=jnp.float32,
    )
    hidden = (jax.nn.silu(gate_part) * up_part).astype(jnp.bfloat16)
    partial_value = jnp.dot(
        hidden,
        lax.all_gather(down_weight, "grp", axis=1, tiled=True),
        preferred_element_type=jnp.float32,
    )
    expert_out = lax.psum_scatter(
        partial_value.astype(jnp.bfloat16), "ep", scatter_dimension=0, tiled=True
    ).astype(jnp.float32)
    token_ids = lax.broadcasted_iota(jnp.int32, (local_tokens, slot_count), 0)
    selector = jnp.where(token_ids == routed_slots[None, :], combine_weight[None, :], 0.0)
    mixed = jnp.dot(
        selector, expert_out, precision=lax.Precision.HIGHEST, preferred_element_type=jnp.float32
    )
    return mixed.astype(jnp.bfloat16)


def solution(mesh):
    placed = (
        P(("grp", "ep"), None),
        P(("grp", "ep")),
        P(("grp", "ep")),
        P("grp", "ep"),
        P("grp", "ep"),
        P("ep", "grp"),
    )
    return jax.shard_map(
        on_device, mesh=mesh, in_specs=placed, out_specs=P(("grp", "ep"), None), check_vma=False
    )
```

profile of v0, /device:TPU:0, one launch (start us, length us, event | category | flops | bytes accessed | tf_op | source)
XLA Modules:
  0.0 344.2 jit_solution(1762212282767024643)
XLA Ops:
  6.5 0.0 copy-start
  6.5 0.0 all-gather.7.cloned.1.call-start
  6.5 0.7 all-gather.7.cloned.1.call-update
  7.3 0.0 all-gather.5.cloned.1.call-start
  7.3 0.7 compare_and_fusion
  8.0 0.0 copy-done
  8.0 1.0 gather_fusion
  9.0 1.0 select_select_fusion
  10.0 0.0 all-gather.5.cloned.1.call-update
  10.0 0.0 all-gather.9.cloned.1.call-start
  10.0 0.7 all-gather.9.cloned.1.call-update
  10.7 0.0 all-gather.11.cloned.1.call-start
  10.8 0.5 all-gather.11.cloned.1.call-update
  11.3 0.0 reduce-scatter.4.cloned.1.call-start
  11.3 41.3 %all-gather.7.cloned.1.call-done = bf16[6144,512]{1,0:T(8,128)(2,1)} async-done(((bf16[768,512]{1,0:T(8,128)(2,1)}), bf16[6144,512]{1,0:T(8,128)(2,1)}) %all-gather.7.cloned.1.call-update) | async-done | bytes 6291472 | tf_op jit(solution)/shard_map/all_gather | solution.py:18
  52.7 84.7 %all-gather.5.cloned.1.call-done = bf16[896,6144]{1,0:T(8,128)(2,1)} async-done(((bf16[56,6144]{1,0:T(8,128)(2,1)}), bf16[896,6144]{1,0:T(8,128)(2,1)}) %all-gather.5.cloned.1.call-update) | async-done | bytes 11010064 | tf_op jit(solution)/shard_map/all_gather | solution.py:15
  137.4 10.4 %fusion.7 = f32[896,512]{1,0:T(8,128)S(1)} fusion(bf16[896,6144]{1,0:T(8,128)(2,1)} %all-gather.5.cloned.1.call-done, bf16[6144,512]{1,0:T(8,128)(2,1)} %all-gather.7.cloned.1.call-done), kind=kOutput, calls=%fused_computation.17 | convolution fusion | flops 5637144576 | bytes 19136512 | tf_op jit(solution)/shard_map/dot_general | solution.py:16
  147.8 32.1 %all-gather.9.cloned.1.call-done = bf16[6144,512]{1,0:T(8,128)(2,1)} async-done(((bf16[768,512]{1,0:T(8,128)(2,1)}), bf16[6144,512]{1,0:T(8,128)(2,1)}) %all-gather.9.cloned.1.call-update) | async-done | bytes 6291472 | tf_op jit(solution)/shard_map/all_gather | solution.py:23
  180.0 42.6 %all-gather.11.cloned.1.call-done = bf16[512,6144]{1,0:T(8,128)(2,1)} async-done(((bf16[512,768]{1,0:T(8,128)(2,1)}), bf16[512,6144]{1,0:T(8,128)(2,1)}) %all-gather.11.cloned.1.call-update) | async-done | bytes 6291472 | tf_op jit(solution)/shard_map/all_gather | solution.py:29
  222.6 20.5 %convolution_convert_fusion = bf16[896,6144]{1,0:T(8,128)(2,1)} fusion(bf16[512,6144]{1,0:T(8,128)(2,1)} %all-gather.11.cloned.1.call-done, f32[896,512]{1,0:T(8,128)S(1)} %fusion.7, bf16[896,6144]{1,0:T(8,128)(2,1)} %all-gather.5.cloned.1.call-done, bf16[6144,512]{1,0:T(8,128)(2,1)} %all-gather.9.cloned.1.call-done), kind=kOutput, calls=%fused_computation.1 | convolution fusion | flops 11282546688 | bytes 36438016 | tf_op jit(solution)/shard_map/dot_general | solution.py:27
  243.1 0.0 copy-start.1
  243.1 0.0 copy-start.2
  243.1 0.0 reduce-scatter.4.cloned.1.call-update
  243.1 90.9 %reduce-scatter.4.cloned.1.call-done = bf16[56,6144]{1,0:T(8,128)(2,1)} async-done(((bf16[896,6144]{1,0:T(8,128)(2,1)}), bf16[56,6144]{1,0:T(8,128)(2,1)}) %reduce-scatter.4.cloned.1.call-update) | async-done | bytes 688144
  334.0 0.0 copy-done.1
  334.0 0.0 copy-done.2
  334.0 3.6 %convolution_convert_fusion.1 = bf16[128,6144]{1,0:T(8,128)(2,1)} fusion(bf16[56,6144]{1,0:T(8,128)(2,1)} %reduce-scatter.4.cloned.1.call-done, f32[56]{0:T(128)S(1)} %copy-done.2, s32[56]{0:T(128)S(1)} %copy-done.1), kind=kOutput, calls=%fused_computation.2 | convolution fusion | flops 529283072 | bytes 2261440 | tf_op jit(solution)/shard_map/dot_general | solution.py:37
  (1 shorter events, 0.0 us)
Async XLA Ops:
  6.5 1.4 copy-start
  6.5 46.1 %all-gather.7.cloned.1.call-start = ((), (), s32[]{:S(2)}) async-start(), calls=%async_computation.2 | async-start | bytes 7077888 | tf_op jit(solution)/shard_map/all_gather | solution.py:18
  7.3 130.1 %all-gather.5.cloned.1.call-start = ((), (), s32[]{:S(2)}) async-start(), calls=%async_computation.1 | async-start | bytes 11698176 | tf_op jit(solution)/shard_map/all_gather | solution.py:15
  10.0 170.0 %all-gather.9.cloned.1.call-start = ((), (), s32[]{:S(2)}) async-start(), calls=%async_computation.3 | async-start | bytes 7077888 | tf_op jit(solution)/shard_map/all_gather | solution.py:23
  10.7 211.9 %all-gather.11.cloned.1.call-start = ((), (), s32[]{:S(2)}) async-start(), calls=%async_computation.4 | async-start | bytes 7077888 | tf_op jit(solution)/shard_map/all_gather | solution.py:29
  11.3 322.7 %reduce-scatter.4.cloned.1.call-start = ((), (), s32[]{:S(2)}) async-start(), calls=%async_computation.5 | async-start | bytes 11698176
  243.1 90.9 %copy-start.1 = (s32[56]{0:T(128)S(1)}, s32[56]{0:T(128)}, u32[]{:S(2)}) copy-start(s32[56]{0:T(128)} %param.7) | copy-start | bytes 676
  243.1 90.9 %copy-start.2 = (f32[56]{0:T(128)S(1)}, f32[56]{0:T(128)}, u32[]{:S(2)}) copy-start(f32[56]{0:T(128)} %param.8) | copy-start | bytes 676
Sparse Core Ops, SparseCore 0:
  9.0 43.5 all-gather.6
  54.8 82.5 all-gather.4
  139.1 40.8 all-gather.8
  181.5 41.0 all-gather.10
  243.3 90.7 reduce-scatter.3
where the time goes:
time: 344 us
  waiting for transfers between devices  294 us (85%)
  matrix products  34.6 us (10%)
  between operations  13.2 us (4%)
    unnamed x6, waiting for transfers between devices  92.8 us
    all_gather x1, waiting for transfers between devices, on_device(): gathered = lax.all_gather(packed, 'ep', axis=0, tiled=True)  84.7 us
    all_gather x1, waiting for transfers between devices, on_device(): lax.all_gather(down_weight, 'grp', axis=1, tiled=True)  42.6 us
    all_gather x1, waiting for transfers between devices, on_device(): lax.all_gather(gate_weight, 'grp', axis=0, tiled=True)  41.3 us
    all_gather x1, waiting for transfers between devices, on_device(): lax.all_gather(up_weight, 'grp', axis=0, tiled=True)  32.1 us
    dot_general x1, matrix products, on_device(): jnp.dot(hidden, lax.all_gather(down_weight, 'grp', axis=1, tiled=True), p...  20.5 us
    dot_general x1, matrix products, on_device(): jnp.dot(gathered, lax.all_gather(gate_weight, 'grp', axis=0, tiled=True),...  10.4 us
  transfers between devices with their start and end apart: 5, of which 5 were waited for; matrix products, arithmetic and copies ran while one was open for 4% of the time, Pallas kernels for 0%

commit v1 on v0

v1 whole, which is shorter than its diff:
```python
import jax
import jax.numpy as jnp
from jax import lax
from jax.experimental import pallas as pl
from jax.experimental.pallas import tpu as pltpu
from jax.sharding import PartitionSpec as P

BOTH = ("grp", "ep")
F32, BF16 = jnp.float32, jnp.bfloat16


def first(core):
    return 1 if core == 0 else 3


def pairs(axis, step):
    out = []
    for g in range(8):
        z, c = divmod(g, 2)
        off = first(c) if step == 0 else 4 - first(c)
        for e in range(16):
            y, x = divmod(e, 4)
            x2 = x ^ off if axis == "x" else x
            y2 = y ^ off if axis == "y" else y
            z2 = z ^ off if axis == "z" else z
            out.append((g * 16 + e, (2 * z2 + c) * 16 + 4 * y2 + x2))
    return out


PAIRS = {axis: (pairs(axis, 0), pairs(axis, 1)) for axis in "xyz"}
SWAP = [(g * 16 + e, (g ^ 1) * 16 + e) for g in range(8) for e in range(16)]


def exchange(value, axis, step):
    return lax.ppermute(value, BOTH, PAIRS[axis][step])


def swap(value):
    return lax.ppermute(value, BOTH, SWAP)


def shard_order():
    table = []
    for g in range(8):
        z, c = divmod(g, 2)
        p = first(c)
        q = 4 - p
        own = [2 * (z ^ o) + c for o in (0, p, q, 2)]
        other = [2 * (z ^ o) + 1 - c for o in (0, q, p, 2)]
        table.append(own[:2] + other[:2] + own[2:] + other[2:])
    return table


def pack(order, routed_slots, tokens):
    cap, width = routed_slots.shape[0], tokens.shape[1] // 8

    def kernel(order_ref, slots_ref, tokens_ref, a_ref, b_ref):
        ids = lax.broadcasted_iota(jnp.int32, (tokens.shape[0], cap), 0)
        pick = (ids == slots_ref[...]).astype(F32).T.astype(BF16)
        for j in range(8):
            start = pl.multiple_of(order_ref[j] * width, 128)
            part = jnp.dot(pick, tokens_ref[:, pl.ds(start, width)], preferred_element_type=F32).astype(BF16)
            target = a_ref if j < 4 else b_ref
            target[:, (j % 4) * width : (j % 4 + 1) * width] = part

    return pl.pallas_call(
        kernel,
        in_specs=[pl.BlockSpec(memory_space=pltpu.SMEM), pl.BlockSpec(memory_space=pltpu.VMEM), pl.BlockSpec(memory_space=pltpu.VMEM)],
        out_specs=[pl.BlockSpec(memory_space=pltpu.VMEM)] * 2,
        out_shape=[jax.ShapeDtypeStruct((cap, 4 * width), BF16)] * 2,
        compiler_params=pltpu.CompilerParams(vmem_limit_bytes=16 * 2**20),
        name="pack",
    )(order, routed_slots.reshape(1, cap), tokens)


def place(order, routed_slots, combine, pieces, tokens_here):
    cap = routed_slots.shape[0]
    width = pieces[0][0].shape[1] // 2

    def kernel(order_ref, slots_ref, combine_ref, *refs):
        out_ref = refs[-1]
        ids = lax.broadcasted_iota(jnp.int32, (tokens_here, cap), 0)
        put = (ids == slots_ref[...]).astype(BF16)
        for k in range(4):
            total = refs[2 * k][...].astype(F32) + refs[2 * k + 1][...].astype(F32)
            value = (combine_ref[...] * total).astype(BF16)
            rows = jnp.dot(put, value, preferred_element_type=F32).astype(BF16)
            for i in range(2):
                start = pl.multiple_of(order_ref[2 * k + i] * width, 128)
                out_ref[:, pl.ds(start, width)] = rows[:, i * width : (i + 1) * width]

    flat = [v for pair in pieces for v in pair]
    return pl.pallas_call(
        kernel,
        in_specs=[pl.BlockSpec(memory_space=pltpu.SMEM)] + [pl.BlockSpec(memory_space=pltpu.VMEM)] * (2 + len(flat)),
        out_specs=pl.BlockSpec(memory_space=pltpu.VMEM),
        out_shape=jax.ShapeDtypeStruct((tokens_here, 8 * width), BF16),
        compiler_params=pltpu.CompilerParams(vmem_limit_bytes=16 * 2**20),
        name="place",
    )(order, routed_slots.reshape(1, cap), combine.reshape(cap, 1), *flat)


def gather_rows(own, axes):
    value = own
    for axis in axes:
        for step in (0, 1):
            got = exchange(value, axis, step)
            if axis == axes[1] and step == 1:
                return value, got
            value = jnp.concatenate([value, got], axis=0)


def dot(a, b):
    return jnp.dot(a, b, preferred_element_type=F32)


def sum_rows(near, far, axes):
    got = exchange(far, axes[0], 1)
    rest = near
    for axis, step in ((axes[0], 0), (axes[1], 1), (axes[1], 0)):
        total = rest + got.astype(F32)
        half = total.shape[0] // 2
        rest = total[:half]
        got = exchange(total[half:].astype(BF16), axis, step)
    return rest, got


def on_device(tokens, routed_slots, combine_weight, gate_weight, up_weight, down_weight):
    cap = routed_slots.shape[0]
    order = jnp.asarray(shard_order(), jnp.int32)[lax.axis_index("grp")]

    both = jnp.concatenate([gate_weight, up_weight], axis=1)
    near_w = jnp.concatenate([both, exchange(both, "z", 0)], axis=0)
    far_w = exchange(near_w, "z", 1)
    near_w2, far_w2 = swap(near_w), swap(far_w)

    own_a, own_b = pack(order, routed_slots, tokens)
    near_a, far_a = gather_rows(own_a, "xy")
    near_b, far_b = gather_rows(own_b, "yx")

    near_d = jnp.concatenate([down_weight, exchange(down_weight, "z", 0)], axis=1)
    far_d = exchange(near_d, "z", 1)
    near_d2, far_d2 = swap(near_d), swap(far_d)

    k = near_w.shape[0]

    def up_sums(rows, w, w2):
        return dot(rows[:, :k], w) + dot(rows[:, k:], w2)

    acc_a = jnp.concatenate([up_sums(near_a, near_w, near_w2), up_sums(far_a, near_w, near_w2)], axis=0)
    acc_b = jnp.concatenate([up_sums(near_b, far_w, far_w2), up_sums(far_b, far_w, far_w2)], axis=0)
    wide = acc_a.shape[1]

    def other_order(v):
        return v.reshape(4, 4, cap, -1).swapaxes(0, 1).reshape(16 * cap, -1)

    acc = acc_a + other_order(acc_b)
    ff = wide // 2
    hidden_a = (jax.nn.silu(acc[:, :ff]) * acc[:, ff:]).astype(BF16)
    hidden_b = other_order(hidden_a)

    half = 8 * cap
    pieces = []
    for w, w2 in ((near_d, near_d2), (far_d, far_d2)):
        for h, wd, axes in ((hidden_a, w, "yx"), (hidden_b, w2, "xy")):
            pieces.append(sum_rows(dot(h[:half], wd), dot(h[half:], wd).astype(BF16), axes))
    return place(order, routed_slots, combine_weight, pieces, tokens.shape[0])


def solution(mesh):
    placed = (
        P(("grp", "ep"), None),
        P(("grp", "ep")),
        P(("grp", "ep")),
        P("grp", "ep"),
        P("grp", "ep"),
        P("ep", "grp"),
    )
    return jax.shard_map(
        on_device, mesh=mesh, in_specs=placed, out_specs=P(("grp", "ep"), None), check_vma=False
    )
```

time: 344 us -> 185 us (0.54)
  waiting for transfers between devices: 294 us -> 106 us
  starting transfers between devices: 0.16 us -> 41.1 us
  matrix products: 34.6 us -> 20 us
  between operations: 13.2 us -> 0.54 us
  local copies, waits for them, and re-layouts: 0.97 us -> 7.43 us
    all_gather x4 -> x0, waiting for transfers between devices: 201 us -> none  [the longest x1 84.7 us: on_device(): gathered = lax.all_gather(packed, 'ep', axis=0, tiled=True)]
    ppermute x0 -> x32, waiting for transfers between devices: none -> 106 us  [the longest x28 106 us: exchange(): return lax.ppermute(value, BOTH, PAIRS[axis][step])]
    unnamed x6 -> x0, waiting for transfers between devices: 92.8 us -> none
    ppermute x0 -> x32, starting transfers between devices: none -> 41.1 us  [the longest x28 40.6 us: exchange(): return lax.ppermute(value, BOTH, PAIRS[axis][step])]
    dot_general x3 -> x16, matrix products: 34.6 us -> 20 us  [dot(): return jnp.dot(a, b, preferred_element_type=F32)]
  transfers between devices with their start and end apart: 5 -> 32, of which waited for: 5 -> 18; matrix products, arithmetic and copies ran while one was open for 4% -> 16% of each run, Pallas kernels for 0% -> 0%
where the time goes in v1:
time: 185 us; the launch traced here: 182 us
  waiting for transfers between devices  106 us (57%)
  starting transfers between devices  41.1 us (22%)
  matrix products  20 us (11%)
  local copies, waits for them, and re-layouts  7.43 us (4%)
  other arithmetic  3.92 us (2%)
  Pallas kernels  3.31 us (2%)
    ppermute x28, waiting for transfers between devices, exchange(): return lax.ppermute(value, BOTH, PAIRS[axis][step])  106 us
    ppermute x28, starting transfers between devices, exchange(): return lax.ppermute(value, BOTH, PAIRS[axis][step])  40.6 us
    dot_general x16, matrix products, dot(): return jnp.dot(a, b, preferred_element_type=F32)  20 us
  transfers between devices with their start and end apart: 32, of which 18 were waited for; matrix products, arithmetic and copies ran while one was open for 16% of the time, Pallas kernels for 0%

profile of v1, /device:TPU:0, one launch (start us, length us, event | category | flops | bytes accessed | tf_op | source)
XLA Modules:
  0.0 182.3 jit_solution(10522552393561718098)
XLA Ops:
  0.0 0.7 dynamic-slice_bitcast_fusion.order_ref
  0.7 1.4 copy-done
  2.1 0.7 copy-done.1
  2.8 1.0 pack.1
  3.7 1.7 collective-permute-start
  5.6 2.0 %collective-permute-start.3 = (bf16[768,1024]{1,0:T(8,128)(2,1)S(1)}, bf16[768,1024]{1,0:T(8,128)(2,1)S(1)}, u32[]{:S(2)}, u32[]{:S(2)}) collective-permute-start(bf16[768,1024]{1,0:T(8,128)(2,1)S(1)} %constant_dynamic-update-slice_fusion.4), channel_id=1, source_target_pairs={{0,32},{1,33},{2,34},{3,35},{4,36},{5,37},{6,38},{7,39},{8,40},{9,... | collective-permute-start | bytes 4718600 | tf_op jit(solution)/shard_map/ppermute | solution.py:35
  7.7 1.6 collective-permute-start.6
  9.3 1.7 collective-permute-done
  11.1 2.9 %collective-permute-start.1 = (bf16[112,3072]{1,0:T(8,128)(2,1)S(1)}, bf16[112,3072]{1,0:T(8,128)(2,1)S(1)}, u32[]{:S(2)}, u32[]{:S(2)}) collective-permute-start(bf16[112,3072]{1,0:T(8,128)(2,1)S(1)} %pad_maximum_fusion.4), channel_id=1, source_target_pairs={{0,3},{1,2},{2,1},{3,0},{4,7},{5,6},{6,5},{7,4},{8,11},{9,10},{10,... | collective-permute-start | bytes 2064392 | tf_op jit(solution)/shard_map/ppermute | solution.py:35
  14.1 0.9 collective-permute-done.6
  15.0 3.1 %collective-permute-start.7 = (bf16[112,3072]{1,0:T(8,128)(2,1)S(1)}, bf16[112,3072]{1,0:T(8,128)(2,1)S(1)}, u32[]{:S(2)}, u32[]{:S(2)}) collective-permute-start(bf16[112,3072]{1,0:T(8,128)(2,1)S(1)} %pad_maximum_fusion.5), channel_id=1, source_target_pairs={{0,12},{1,13},{2,14},{3,15},{4,8},{5,9},{6,10},{7,11},{8,4},{9,5},... | collective-permute-start | bytes 2064392 | tf_op jit(solution)/shard_map/ppermute | solution.py:35
  18.1 5.3 %collective-permute-done.1 = bf16[112,3072]{1,0:T(8,128)(2,1)S(1)} collective-permute-done((bf16[112,3072]{1,0:T(8,128)(2,1)S(1)}, bf16[112,3072]{1,0:T(8,128)(2,1)S(1)}, u32[]{:S(2)}, u32[]{:S(2)}) %collective-permute-start.1) | collective-permute-done | bytes 688160 | tf_op jit(solution)/shard_map/ppermute | solution.py:35
  23.5 1.7 collective-permute-start.2
  25.2 0.9 collective-permute-done.3
  26.4 4.1 %collective-permute-start.9 = (bf16[1536,1024]{1,0:T(8,128)(2,1)S(1)}, bf16[1536,1024]{1,0:T(8,128)(2,1)S(1)}, u32[]{:S(2)}, u32[]{:S(2)}) collective-permute-start(bf16[1536,1024]{1,0:T(8,128)(2,1)S(1)} %pad_maximum_fusion.1), channel_id=1, source_target_pairs={{0,96},{1,97},{2,98},{3,99},{4,100},{5,101},{6,102},{7,103},{8,104... | collective-permute-start | bytes 9437192 | tf_op jit(solution)/shard_map/ppermute | solution.py:35
  30.7 0.6 collective-permute-start.8
  31.3 7.7 %collective-permute-done.12 = bf16[512,768]{1,0:T(8,128)(2,1)S(1)} collective-permute-done((bf16[512,768]{1,0:T(8,128)(2,1)S(1)}, bf16[512,768]{1,0:T(8,128)(2,1)S(1)}, u32[]{:S(2)}, u32[]{:S(2)}) %collective-permute-start.12) | collective-permute-done | bytes 786464 | tf_op jit(solution)/shard_map/ppermute | solution.py:35
  39.0 3.9 %collective-permute-start.22 = (bf16[512,1536]{1,0:T(8,128)(2,1)S(1)}, bf16[512,1536]{1,0:T(8,128)(2,1)S(1)}, u32[]{:S(2)}, u32[]{:S(2)}) collective-permute-start(bf16[512,1536]{1,0:T(8,128)(2,1)S(1)} %constant_dynamic-update-slice_fusion.10), channel_id=1, source_target_pairs={{0,96},{1,97},{2,98},{3,99},{4,100},{5,101},{6,102},{7,103},{8,104... | collective-permute-start | bytes 4718600 | tf_op jit(solution)/shard_map/ppermute | solution.py:35
  43.1 3.1 %collective-permute-start.5 = (bf16[448,3072]{1,0:T(8,128)(2,1)S(1)}, bf16[448,3072]{1,0:T(8,128)(2,1)S(1)}, u32[]{:S(2)}, u32[]{:S(2)}) collective-permute-start(bf16[448,3072]{1,0:T(8,128)(2,1)S(1)} %constant_dynamic-update-slice_fusion), channel_id=1, source_target_pairs={{0,12},{1,13},{2,14},{3,15},{4,8},{5,9},{6,10},{7,11},{8,4},{9,5},... | collective-permute-start | bytes 8257544 | tf_op jit(solution)/shard_map/ppermute | solution.py:35
  46.2 2.8 %collective-permute-done.8 = bf16[224,3072]{1,0:T(8,128)(2,1)S(1)} collective-permute-done((bf16[224,3072]{1,0:T(8,128)(2,1)S(1)}, bf16[224,3072]{1,0:T(8,128)(2,1)S(1)}, u32[]{:S(2)}, u32[]{:S(2)}) %collective-permute-start.8) | collective-permute-done | bytes 1376288 | tf_op jit(solution)/shard_map/ppermute | solution.py:35
  49.2 2.2 %collective-permute-start.11 = (bf16[448,3072]{1,0:T(8,128)(2,1)S(1)}, bf16[448,3072]{1,0:T(8,128)(2,1)S(1)}, u32[]{:S(2)}, u32[]{:S(2)}) collective-permute-start(bf16[448,3072]{1,0:T(8,128)(2,1)S(1)} %constant_dynamic-update-slice_fusion.6), channel_id=1, source_target_pairs={{0,3},{1,2},{2,1},{3,0},{4,7},{5,6},{6,5},{7,4},{8,11},{9,10},{10,... | collective-permute-start | bytes 8257544 | tf_op jit(solution)/shard_map/ppermute | solution.py:35
  51.3 19.1 %collective-permute-done.9 = bf16[1536,1024]{1,0:T(8,128)(2,1)S(1)} collective-permute-done((bf16[1536,1024]{1,0:T(8,128)(2,1)S(1)}, bf16[1536,1024]{1,0:T(8,128)(2,1)S(1)}, u32[]{:S(2)}, u32[]{:S(2)}) %collective-permute-start.9) | collective-permute-done | bytes 3145760 | tf_op jit(solution)/shard_map/ppermute | solution.py:35
  70.4 1.6 fusion.5
  72.0 15.2 %collective-permute-done.22 = bf16[512,1536]{1,0:T(8,128)(2,1)S(1)} collective-permute-done((bf16[512,1536]{1,0:T(8,128)(2,1)S(1)}, bf16[512,1536]{1,0:T(8,128)(2,1)S(1)}, u32[]{:S(2)}, u32[]{:S(2)}) %collective-permute-start.22) | collective-permute-done | bytes 1572896 | tf_op jit(solution)/shard_map/ppermute | solution.py:35
  87.2 0.5 collective-permute-start.27
  87.7 1.6 fusion.10
  89.3 1.6 convolution_add_fusion.7
  91.0 1.6 fusion.7
  92.6 1.6 fusion.2
  94.2 1.6 convolution_add_fusion.6
  95.9 1.6 convolution_add_fusion.4
  97.5 1.6 convolution_add_fusion.5
  100.1 1.2 maximum_add_fusion
  101.3 0.6 fusion
  101.9 0.9 convolution_convert_fusion.3
  102.8 3.1 %collective-permute-start.13 = (bf16[448,1536]{1,0:T(8,128)(2,1)S(1)}, bf16[448,1536]{1,0:T(8,128)(2,1)S(1)}, u32[]{:S(2)}, u32[]{:S(2)}) collective-permute-start(bf16[448,1536]{1,0:T(8,128)(2,1)S(1)} %convolution_convert_fusion.3), channel_id=1, source_target_pairs={{0,12},{1,13},{2,14},{3,15},{4,8},{5,9},{6,10},{7,11},{8,4},{9,5},... | collective-permute-start | bytes 4128776 | tf_op jit(solution)/shard_map/ppermute | solution.py:35
  106.1 0.9 convolution_convert_fusion.2
  107.0 0.8 collective-permute-start.18
  107.8 0.9 convolution_convert_fusion.1
  109.0 0.9 convolution_convert_fusion
  109.8 2.8 %collective-permute-start.28 = (bf16[448,1536]{1,0:T(8,128)(2,1)S(1)}, bf16[448,1536]{1,0:T(8,128)(2,1)S(1)}, u32[]{:S(2)}, u32[]{:S(2)}) collective-permute-start(bf16[448,1536]{1,0:T(8,128)(2,1)S(1)} %convolution_convert_fusion), channel_id=1, source_target_pairs={{0,3},{1,2},{2,1},{3,0},{4,7},{5,6},{6,5},{7,4},{8,11},{9,10},{10,... | collective-permute-start | bytes 4128776 | tf_op jit(solution)/shard_map/ppermute | solution.py:35
  112.7 9.8 %collective-permute-done.13 = bf16[448,1536]{1,0:T(8,128)(2,1)S(1)} collective-permute-done((bf16[448,1536]{1,0:T(8,128)(2,1)S(1)}, bf16[448,1536]{1,0:T(8,128)(2,1)S(1)}, u32[]{:S(2)}, u32[]{:S(2)}) %collective-permute-start.13) | collective-permute-done | bytes 1376288 | tf_op jit(solution)/shard_map/ppermute | solution.py:35
  122.4 0.9 convolution_add_fusion.3
  123.8 3.0 %collective-permute-done.18 = bf16[448,1536]{1,0:T(8,128)(2,1)S(1)} collective-permute-done((bf16[448,1536]{1,0:T(8,128)(2,1)S(1)}, bf16[448,1536]{1,0:T(8,128)(2,1)S(1)}, u32[]{:S(2)}, u32[]{:S(2)}) %collective-permute-start.18) | collective-permute-done | bytes 1376288 | tf_op jit(solution)/shard_map/ppermute | solution.py:35
  126.8 0.9 convolution_add_fusion.2
  127.9 16.7 %collective-permute-done.23 = bf16[448,1536]{1,0:T(8,128)(2,1)S(1)} collective-permute-done((bf16[448,1536]{1,0:T(8,128)(2,1)S(1)}, bf16[448,1536]{1,0:T(8,128)(2,1)S(1)}, u32[]{:S(2)}, u32[]{:S(2)}) %collective-permute-start.23) | collective-permute-done | bytes 1376288 | tf_op jit(solution)/shard_map/ppermute | solution.py:35
  144.5 0.9 convolution_add_fusion.1
  145.9 3.0 %collective-permute-done.28 = bf16[448,1536]{1,0:T(8,128)(2,1)S(1)} collective-permute-done((bf16[448,1536]{1,0:T(8,128)(2,1)S(1)}, bf16[448,1536]{1,0:T(8,128)(2,1)S(1)}, u32[]{:S(2)}, u32[]{:S(2)}) %collective-permute-start.28) | collective-permute-done | bytes 1376288 | tf_op jit(solution)/shard_map/ppermute | solution.py:35
  148.9 0.9 convolution_add_fusion
  150.2 0.6 collective-permute-start.15
  151.0 0.6 collective-permute-start.20
  151.7 8.5 %collective-permute-done.24 = bf16[224,1536]{1,0:T(8,128)(2,1)S(1)} collective-permute-done((bf16[224,1536]{1,0:T(8,128)(2,1)S(1)}, bf16[224,1536]{1,0:T(8,128)(2,1)S(1)}, u32[]{:S(2)}, u32[]{:S(2)}) %collective-permute-start.24) | collective-permute-done | bytes 688160 | tf_op jit(solution)/shard_map/ppermute | solution.py:35
  160.7 3.9 %collective-permute-done.29 = bf16[224,1536]{1,0:T(8,128)(2,1)S(1)} collective-permute-done((bf16[224,1536]{1,0:T(8,128)(2,1)S(1)}, bf16[224,1536]{1,0:T(8,128)(2,1)S(1)}, u32[]{:S(2)}, u32[]{:S(2)}) %collective-permute-start.29) | collective-permute-done | bytes 688160 | tf_op jit(solution)/shard_map/ppermute | solution.py:35
  165.1 0.7 slice.273
  166.1 0.7 slice.272
  166.8 2.0 %collective-permute-start.21 = (bf16[56,1536]{1,0:T(8,128)(2,1)}, bf16[56,1536]{1,0:T(8,128)(2,1)S(1)}, u32[]{:S(2)}, u32[]{:S(2)}) collective-permute-start(bf16[56,1536]{1,0:T(8,128)(2,1)} %slice.272), channel_id=1, source_target_pairs={{0,4},{1,5},{2,6},{3,7},{4,0},{5,1},{6,2},{7,3},{8,12},{9,13},{10,... | collective-permute-start | bytes 516104 | tf_op jit(solution)/shard_map/ppermute | solution.py:35
  168.8 2.0 %collective-permute-done.25 = bf16[112,1536]{1,0:T(8,128)(2,1)S(1)} collective-permute-done((bf16[112,1536]{1,0:T(8,128)(2,1)S(1)}, bf16[112,1536]{1,0:T(8,128)(2,1)S(1)}, u32[]{:S(2)}, u32[]{:S(2)}) %collective-permute-start.25) | collective-permute-done | bytes 344096 | tf_op jit(solution)/shard_map/ppermute | solution.py:35
  170.9 0.7 slice.271
  171.6 1.9 %collective-permute-done.30 = bf16[112,1536]{1,0:T(8,128)(2,1)S(1)} collective-permute-done((bf16[112,1536]{1,0:T(8,128)(2,1)S(1)}, bf16[112,1536]{1,0:T(8,128)(2,1)S(1)}, u32[]{:S(2)}, u32[]{:S(2)}) %collective-permute-start.30) | collective-permute-done | bytes 344096 | tf_op jit(solution)/shard_map/ppermute | solution.py:35
  173.6 0.7 slice.270
  174.3 1.7 collective-permute-start.31
  176.3 1.0 collective-permute-done.26.refs_5_
  177.3 2.7 %collective-permute-done.31.refs_7_ = bf16[56,1536]{1,0:T(8,128)(2,1)S(1)} collective-permute-done((bf16[56,1536]{1,0:T(8,128)(2,1)}, bf16[56,1536]{1,0:T(8,128)(2,1)S(1)}, u32[]{:S(2)}, u32[]{:S(2)}) %collective-permute-start.31) | collective-permute-done | bytes 172064 | tf_op jit(solution)/shard_map/ppermute | solution.py:35
  180.0 2.3 %place.1 = bf16[128,6144]{1,0:T(8,128)(2,1)} custom-call(s32[8]{0:T(128)S(1)} %dynamic-slice_bitcast_fusion.order_ref, s32[1,56]{1,0:T(1,128)S(1)} %bitcast.34, f32[56,1]{1,0:T(8,128)S(1)} %copy.12.combine_ref, f32[56,1536]{1,0:T(8,128)S(1)} %slice.192.refs_0_, bf16[56,1536]{1,0:T(8,128)(2,1)S(1)} %collective-permute-done.16.refs_1_, ...), custom_call_target="tpu_custom_call" | custom-call | tf_op jit(solution)/shard_map/place/pallas_call | solution.py:93
  (80 shorter events, 6.2 us)
Async XLA Ops:
  0.7 1.4 copy-start
  2.1 0.7 copy-start.1
  2.8 2.6 %copy-start.3 = (bf16[768,512]{1,0:T(8,128)(2,1)S(1)}, bf16[768,512]{1,0:T(8,128)(2,1)}, u32[]{:S(2)}) copy-start(bf16[768,512]{1,0:T(8,128)(2,1)} %param.10) | copy-start | bytes 2359300
  2.8 2.7 %copy-start.4 = (bf16[768,512]{1,0:T(8,128)(2,1)S(1)}, bf16[768,512]{1,0:T(8,128)(2,1)}, u32[]{:S(2)}) copy-start(bf16[768,512]{1,0:T(8,128)(2,1)} %param.11) | copy-start | bytes 2359300
  3.7 3.9 %copy-start.5 = (bf16[512,768]{1,0:T(8,128)(2,1)S(1)}, bf16[512,768]{1,0:T(8,128)(2,1)}, u32[]{:S(2)}) copy-start(bf16[512,768]{1,0:T(8,128)(2,1)} %param.12) | copy-start | bytes 2359300
  3.7 7.3 %collective-permute-start = (bf16[56,3072]{1,0:T(8,128)(2,1)S(1)}, bf16[56,3072]{1,0:T(8,128)(2,1)S(1)}, u32[]{:S(2)}, u32[]{:S(2)}) collective-permute-start(bf16[56,3072]{1,0:T(8,128)(2,1)S(1)} %get-tuple-element.7), channel_id=1, source_target_pairs={{0,1},{1,0},{2,3},{3,2},{4,5},{5,4},{6,7},{7,6},{8,9},{9,8},{10,11... | collective-permute-start | bytes 1032200 | tf_op jit(solution)/shard_map/ppermute | solution.py:35
  5.6 20.5 %collective-permute-start.3 = (bf16[768,1024]{1,0:T(8,128)(2,1)S(1)}, bf16[768,1024]{1,0:T(8,128)(2,1)S(1)}, u32[]{:S(2)}, u32[]{:S(2)}) collective-permute-start(bf16[768,1024]{1,0:T(8,128)(2,1)S(1)} %constant_dynamic-update-slice_fusion.4), channel_id=1, source_target_pairs={{0,32},{1,33},{2,34},{3,35},{4,36},{5,37},{6,38},{7,39},{8,40},{9,... | collective-permute-start | bytes 4718600 | tf_op jit(solution)/shard_map/ppermute | solution.py:35
  7.6 31.4 %collective-permute-start.12 = (bf16[512,768]{1,0:T(8,128)(2,1)S(1)}, bf16[512,768]{1,0:T(8,128)(2,1)S(1)}, u32[]{:S(2)}, u32[]{:S(2)}) collective-permute-start(bf16[512,768]{1,0:T(8,128)(2,1)S(1)} %copy-done.5), channel_id=1, source_target_pairs={{0,32},{1,33},{2,34},{3,35},{4,36},{5,37},{6,38},{7,39},{8,40},{9,... | collective-permute-start | bytes 2359304 | tf_op jit(solution)/shard_map/ppermute | solution.py:35
  7.7 7.2 %collective-permute-start.6 = (bf16[56,3072]{1,0:T(8,128)(2,1)S(1)}, bf16[56,3072]{1,0:T(8,128)(2,1)S(1)}, u32[]{:S(2)}, u32[]{:S(2)}) collective-permute-start(bf16[56,3072]{1,0:T(8,128)(2,1)S(1)} %get-tuple-element.8), channel_id=1, source_target_pairs={{0,4},{1,5},{2,6},{3,7},{4,0},{5,1},{6,2},{7,3},{8,12},{9,13},{10,... | collective-permute-start | bytes 1032200 | tf_op jit(solution)/shard_map/ppermute | solution.py:35
  11.1 12.2 %collective-permute-start.1 = (bf16[112,3072]{1,0:T(8,128)(2,1)S(1)}, bf16[112,3072]{1,0:T(8,128)(2,1)S(1)}, u32[]{:S(2)}, u32[]{:S(2)}) collective-permute-start(bf16[112,3072]{1,0:T(8,128)(2,1)S(1)} %pad_maximum_fusion.4), channel_id=1, source_target_pairs={{0,3},{1,2},{2,1},{3,0},{4,7},{5,6},{6,5},{7,4},{8,11},{9,10},{10,... | collective-permute-start | bytes 2064392 | tf_op jit(solution)/shard_map/ppermute | solution.py:35
  15.0 15.5 %collective-permute-start.7 = (bf16[112,3072]{1,0:T(8,128)(2,1)S(1)}, bf16[112,3072]{1,0:T(8,128)(2,1)S(1)}, u32[]{:S(2)}, u32[]{:S(2)}) collective-permute-start(bf16[112,3072]{1,0:T(8,128)(2,1)S(1)} %pad_maximum_fusion.5), channel_id=1, source_target_pairs={{0,12},{1,13},{2,14},{3,15},{4,8},{5,9},{6,10},{7,11},{8,4},{9,5},... | collective-permute-start | bytes 2064392 | tf_op jit(solution)/shard_map/ppermute | solution.py:35
  23.5 19.5 %collective-permute-start.2 = (bf16[224,3072]{1,0:T(8,128)(2,1)S(1)}, bf16[224,3072]{1,0:T(8,128)(2,1)S(1)}, u32[]{:S(2)}, u32[]{:S(2)}) collective-permute-start(bf16[224,3072]{1,0:T(8,128)(2,1)S(1)} %pad_maximum_fusion.2), channel_id=1, source_target_pairs={{0,4},{1,5},{2,6},{3,7},{4,0},{5,1},{6,2},{7,3},{8,12},{9,13},{10,... | collective-permute-start | bytes 4128776 | tf_op jit(solution)/shard_map/ppermute | solution.py:35
  26.4 44.0 %collective-permute-start.9 = (bf16[1536,1024]{1,0:T(8,128)(2,1)S(1)}, bf16[1536,1024]{1,0:T(8,128)(2,1)S(1)}, u32[]{:S(2)}, u32[]{:S(2)}) collective-permute-start(bf16[1536,1024]{1,0:T(8,128)(2,1)S(1)} %pad_maximum_fusion.1), channel_id=1, source_target_pairs={{0,96},{1,97},{2,98},{3,99},{4,100},{5,101},{6,102},{7,103},{8,104... | collective-permute-start | bytes 9437192 | tf_op jit(solution)/shard_map/ppermute | solution.py:35
  30.7 18.4 %collective-permute-start.8 = (bf16[224,3072]{1,0:T(8,128)(2,1)S(1)}, bf16[224,3072]{1,0:T(8,128)(2,1)S(1)}, u32[]{:S(2)}, u32[]{:S(2)}) collective-permute-start(bf16[224,3072]{1,0:T(8,128)(2,1)S(1)} %pad_maximum_fusion.3), channel_id=1, source_target_pairs={{0,1},{1,0},{2,3},{3,2},{4,5},{5,4},{6,7},{7,6},{8,9},{9,8},{10,11... | collective-permute-start | bytes 4128776 | tf_op jit(solution)/shard_map/ppermute | solution.py:35
  31.3 56.0 %collective-permute-start.4 = (bf16[1536,1024]{1,0:T(8,128)(2,1)S(1)}, bf16[1536,1024]{1,0:T(8,128)(2,1)S(1)}, u32[]{:S(2)}, u32[]{:S(2)}) collective-permute-start(bf16[1536,1024]{1,0:T(8,128)(2,1)S(1)} %pad_maximum_fusion.1), channel_id=1, source_target_pairs={{0,16},{1,17},{2,18},{3,19},{4,20},{5,21},{6,22},{7,23},{8,24},{9,... | collective-permute-start | bytes 9437192 | tf_op jit(solution)/shard_map/ppermute | solution.py:39
  39.0 48.2 %collective-permute-start.22 = (bf16[512,1536]{1,0:T(8,128)(2,1)S(1)}, bf16[512,1536]{1,0:T(8,128)(2,1)S(1)}, u32[]{:S(2)}, u32[]{:S(2)}) collective-permute-start(bf16[512,1536]{1,0:T(8,128)(2,1)S(1)} %constant_dynamic-update-slice_fusion.10), channel_id=1, source_target_pairs={{0,96},{1,97},{2,98},{3,99},{4,100},{5,101},{6,102},{7,103},{8,104... | collective-permute-start | bytes 4718600 | tf_op jit(solution)/shard_map/ppermute | solution.py:35
  43.1 47.9 %collective-permute-start.5 = (bf16[448,3072]{1,0:T(8,128)(2,1)S(1)}, bf16[448,3072]{1,0:T(8,128)(2,1)S(1)}, u32[]{:S(2)}, u32[]{:S(2)}) collective-permute-start(bf16[448,3072]{1,0:T(8,128)(2,1)S(1)} %constant_dynamic-update-slice_fusion), channel_id=1, source_target_pairs={{0,12},{1,13},{2,14},{3,15},{4,8},{5,9},{6,10},{7,11},{8,4},{9,5},... | collective-permute-start | bytes 8257544 | tf_op jit(solution)/shard_map/ppermute | solution.py:35
  49.2 43.5 %collective-permute-start.11 = (bf16[448,3072]{1,0:T(8,128)(2,1)S(1)}, bf16[448,3072]{1,0:T(8,128)(2,1)S(1)}, u32[]{:S(2)}, u32[]{:S(2)}) collective-permute-start(bf16[448,3072]{1,0:T(8,128)(2,1)S(1)} %constant_dynamic-update-slice_fusion.6), channel_id=1, source_target_pairs={{0,3},{1,2},{2,1},{3,0},{4,7},{5,6},{6,5},{7,4},{8,11},{9,10},{10,... | collective-permute-start | bytes 8257544 | tf_op jit(solution)/shard_map/ppermute | solution.py:35
  70.4 25.5 %collective-permute-start.10 = (bf16[1536,1024]{1,0:T(8,128)(2,1)S(1)}, bf16[1536,1024]{1,0:T(8,128)(2,1)S(1)}, u32[]{:S(2)}, u32[]{:S(2)}) collective-permute-start(bf16[1536,1024]{1,0:T(8,128)(2,1)S(1)} %collective-permute-done.9), channel_id=1, source_target_pairs={{0,16},{1,17},{2,18},{3,19},{4,20},{5,21},{6,22},{7,23},{8,24},{9,... | collective-permute-start | bytes 9437192 | tf_op jit(solution)/shard_map/ppermute | solution.py:39
  87.2 18.9 %collective-permute-start.17 = (bf16[512,1536]{1,0:T(8,128)(2,1)S(1)}, bf16[512,1536]{1,0:T(8,128)(2,1)S(1)}, u32[]{:S(2)}, u32[]{:S(2)}) collective-permute-start(bf16[512,1536]{1,0:T(8,128)(2,1)S(1)} %constant_dynamic-update-slice_fusion.10), channel_id=1, source_target_pairs={{0,16},{1,17},{2,18},{3,19},{4,20},{5,21},{6,22},{7,23},{8,24},{9,... | collective-permute-start | bytes 4718600 | tf_op jit(solution)/shard_map/ppermute | solution.py:39
  87.2 21.7 %collective-permute-start.27 = (bf16[512,1536]{1,0:T(8,128)(2,1)S(1)}, bf16[512,1536]{1,0:T(8,128)(2,1)S(1)}, u32[]{:S(2)}, u32[]{:S(2)}) collective-permute-start(bf16[512,1536]{1,0:T(8,128)(2,1)S(1)} %collective-permute-done.22), channel_id=1, source_target_pairs={{0,16},{1,17},{2,18},{3,19},{4,20},{5,21},{6,22},{7,23},{8,24},{9,... | collective-permute-start | bytes 4718600 | tf_op jit(solution)/shard_map/ppermute | solution.py:39
  102.8 19.6 %collective-permute-start.13 = (bf16[448,1536]{1,0:T(8,128)(2,1)S(1)}, bf16[448,1536]{1,0:T(8,128)(2,1)S(1)}, u32[]{:S(2)}, u32[]{:S(2)}) collective-permute-start(bf16[448,1536]{1,0:T(8,128)(2,1)S(1)} %convolution_convert_fusion.3), channel_id=1, source_target_pairs={{0,12},{1,13},{2,14},{3,15},{4,8},{5,9},{6,10},{7,11},{8,4},{9,5},... | collective-permute-start | bytes 4128776 | tf_op jit(solution)/shard_map/ppermute | solution.py:35
  107.0 19.8 %collective-permute-start.18 = (bf16[448,1536]{1,0:T(8,128)(2,1)S(1)}, bf16[448,1536]{1,0:T(8,128)(2,1)S(1)}, u32[]{:S(2)}, u32[]{:S(2)}) collective-permute-start(bf16[448,1536]{1,0:T(8,128)(2,1)S(1)} %convolution_convert_fusion.2), channel_id=1, source_target_pairs={{0,3},{1,2},{2,1},{3,0},{4,7},{5,6},{6,5},{7,4},{8,11},{9,10},{10,... | collective-permute-start | bytes 4128776 | tf_op jit(solution)/shard_map/ppermute | solution.py:35
  108.6 35.9 %collective-permute-start.23 = (bf16[448,1536]{1,0:T(8,128)(2,1)S(1)}, bf16[448,1536]{1,0:T(8,128)(2,1)S(1)}, u32[]{:S(2)}, u32[]{:S(2)}) collective-permute-start(bf16[448,1536]{1,0:T(8,128)(2,1)S(1)} %convolution_convert_fusion.1), channel_id=1, source_target_pairs={{0,12},{1,13},{2,14},{3,15},{4,8},{5,9},{6,10},{7,11},{8,4},{9,5},... | collective-permute-start | bytes 4128776 | tf_op jit(solution)/shard_map/ppermute | solution.py:35
  109.8 39.1 %collective-permute-start.28 = (bf16[448,1536]{1,0:T(8,128)(2,1)S(1)}, bf16[448,1536]{1,0:T(8,128)(2,1)S(1)}, u32[]{:S(2)}, u32[]{:S(2)}) collective-permute-start(bf16[448,1536]{1,0:T(8,128)(2,1)S(1)} %convolution_convert_fusion), channel_id=1, source_target_pairs={{0,3},{1,2},{2,1},{3,0},{4,7},{5,6},{6,5},{7,4},{8,11},{9,10},{10,... | collective-permute-start | bytes 4128776 | tf_op jit(solution)/shard_map/ppermute | solution.py:35
  123.4 26.6 %collective-permute-start.14 = (bf16[224,1536]{1,0:T(8,128)(2,1)S(1)}, bf16[224,1536]{1,0:T(8,128)(2,1)S(1)}, u32[]{:S(2)}, u32[]{:S(2)}) collective-permute-start(bf16[224,1536]{1,0:T(8,128)(2,1)S(1)} %slice.265), channel_id=1, source_target_pairs={{0,4},{1,5},{2,6},{3,7},{4,0},{5,1},{6,2},{7,3},{8,12},{9,13},{10,... | collective-permute-start | bytes 2064392 | tf_op jit(solution)/shard_map/ppermute | solution.py:35
  127.8 23.0 %collective-permute-start.19 = (bf16[224,1536]{1,0:T(8,128)(2,1)S(1)}, bf16[224,1536]{1,0:T(8,128)(2,1)S(1)}, u32[]{:S(2)}, u32[]{:S(2)}) collective-permute-start(bf16[224,1536]{1,0:T(8,128)(2,1)S(1)} %slice.264), channel_id=1, source_target_pairs={{0,1},{1,0},{2,3},{3,2},{4,5},{5,4},{6,7},{7,6},{8,9},{9,8},{10,11... | collective-permute-start | bytes 2064392 | tf_op jit(solution)/shard_map/ppermute | solution.py:35
  145.5 14.7 %collective-permute-start.24 = (bf16[224,1536]{1,0:T(8,128)(2,1)S(1)}, bf16[224,1536]{1,0:T(8,128)(2,1)S(1)}, u32[]{:S(2)}, u32[]{:S(2)}) collective-permute-start(bf16[224,1536]{1,0:T(8,128)(2,1)S(1)} %slice.263), channel_id=1, source_target_pairs={{0,4},{1,5},{2,6},{3,7},{4,0},{5,1},{6,2},{7,3},{8,12},{9,13},{10,... | collective-permute-start | bytes 2064392 | tf_op jit(solution)/shard_map/ppermute | solution.py:35
  149.9 14.8 %collective-permute-start.29 = (bf16[224,1536]{1,0:T(8,128)(2,1)S(1)}, bf16[224,1536]{1,0:T(8,128)(2,1)S(1)}, u32[]{:S(2)}, u32[]{:S(2)}) collective-permute-start(bf16[224,1536]{1,0:T(8,128)(2,1)S(1)} %slice.262), channel_id=1, source_target_pairs={{0,1},{1,0},{2,3},{3,2},{4,5},{5,4},{6,7},{7,6},{8,9},{9,8},{10,11... | collective-permute-start | bytes 2064392 | tf_op jit(solution)/shard_map/ppermute | solution.py:35
  150.2 14.7 %collective-permute-start.15 = (bf16[112,1536]{1,0:T(8,128)(2,1)S(1)}, bf16[112,1536]{1,0:T(8,128)(2,1)S(1)}, u32[]{:S(2)}, u32[]{:S(2)}) collective-permute-start(bf16[112,1536]{1,0:T(8,128)(2,1)S(1)} %slice.269), channel_id=1, source_target_pairs={{0,3},{1,2},{2,1},{3,0},{4,7},{5,6},{6,5},{7,4},{8,11},{9,10},{10,... | collective-permute-start | bytes 1032200 | tf_op jit(solution)/shard_map/ppermute | solution.py:35
  151.0 15.0 %collective-permute-start.20 = (bf16[112,1536]{1,0:T(8,128)(2,1)S(1)}, bf16[112,1536]{1,0:T(8,128)(2,1)S(1)}, u32[]{:S(2)}, u32[]{:S(2)}) collective-permute-start(bf16[112,1536]{1,0:T(8,128)(2,1)S(1)} %slice.268), channel_id=1, source_target_pairs={{0,12},{1,13},{2,14},{3,15},{4,8},{5,9},{6,10},{7,11},{8,4},{9,5},... | collective-permute-start | bytes 1032200 | tf_op jit(solution)/shard_map/ppermute | solution.py:35
  160.4 10.4 %collective-permute-start.25 = (bf16[112,1536]{1,0:T(8,128)(2,1)S(1)}, bf16[112,1536]{1,0:T(8,128)(2,1)S(1)}, u32[]{:S(2)}, u32[]{:S(2)}) collective-permute-start(bf16[112,1536]{1,0:T(8,128)(2,1)S(1)} %slice.267), channel_id=1, source_target_pairs={{0,3},{1,2},{2,1},{3,0},{4,7},{5,6},{6,5},{7,4},{8,11},{9,10},{10,... | collective-permute-start | bytes 1032200 | tf_op jit(solution)/shard_map/ppermute | solution.py:35
  164.9 8.7 %collective-permute-start.30 = (bf16[112,1536]{1,0:T(8,128)(2,1)S(1)}, bf16[112,1536]{1,0:T(8,128)(2,1)S(1)}, u32[]{:S(2)}, u32[]{:S(2)}) collective-permute-start(bf16[112,1536]{1,0:T(8,128)(2,1)S(1)} %slice.266), channel_id=1, source_target_pairs={{0,12},{1,13},{2,14},{3,15},{4,8},{5,9},{6,10},{7,11},{8,4},{9,5},... | collective-permute-start | bytes 1032200 | tf_op jit(solution)/shard_map/ppermute | solution.py:35
  165.7 10.5 %collective-permute-start.16 = (bf16[56,1536]{1,0:T(8,128)(2,1)}, bf16[56,1536]{1,0:T(8,128)(2,1)S(1)}, u32[]{:S(2)}, u32[]{:S(2)}) collective-permute-start(bf16[56,1536]{1,0:T(8,128)(2,1)} %slice.273), channel_id=1, source_target_pairs={{0,1},{1,0},{2,3},{3,2},{4,5},{5,4},{6,7},{7,6},{8,9},{9,8},{10,11... | collective-permute-start | bytes 516104 | tf_op jit(solution)/shard_map/ppermute | solution.py:35
  166.8 9.2 %copy-start.6 = (f32[56]{0:T(128)S(1)}, f32[56]{0:T(128)}, u32[]{:S(2)}) copy-start(f32[56]{0:T(128)} %param.9) | copy-start | bytes 676
  166.8 9.4 %collective-permute-start.21 = (bf16[56,1536]{1,0:T(8,128)(2,1)}, bf16[56,1536]{1,0:T(8,128)(2,1)S(1)}, u32[]{:S(2)}, u32[]{:S(2)}) collective-permute-start(bf16[56,1536]{1,0:T(8,128)(2,1)} %slice.272), channel_id=1, source_target_pairs={{0,4},{1,5},{2,6},{3,7},{4,0},{5,1},{6,2},{7,3},{8,12},{9,13},{10,... | collective-permute-start | bytes 516104 | tf_op jit(solution)/shard_map/ppermute | solution.py:35
  171.6 5.6 %collective-permute-start.26 = (bf16[56,1536]{1,0:T(8,128)(2,1)}, bf16[56,1536]{1,0:T(8,128)(2,1)S(1)}, u32[]{:S(2)}, u32[]{:S(2)}) collective-permute-start(bf16[56,1536]{1,0:T(8,128)(2,1)} %slice.271), channel_id=1, source_target_pairs={{0,1},{1,0},{2,3},{3,2},{4,5},{5,4},{6,7},{7,6},{8,9},{9,8},{10,11... | collective-permute-start | bytes 516104 | tf_op jit(solution)/shard_map/ppermute | solution.py:35
  173.6 6.3 %copy-start.2 = (s32[56]{0:T(128)S(1)}, s32[56]{0:T(128)}, u32[]{:S(2)}) copy-start(s32[56]{0:T(128)} %param.8) | copy-start | bytes 676
  174.3 5.6 %collective-permute-start.31 = (bf16[56,1536]{1,0:T(8,128)(2,1)}, bf16[56,1536]{1,0:T(8,128)(2,1)S(1)}, u32[]{:S(2)}, u32[]{:S(2)}) collective-permute-start(bf16[56,1536]{1,0:T(8,128)(2,1)} %slice.270), channel_id=1, source_target_pairs={{0,4},{1,5},{2,6},{3,7},{4,0},{5,1},{6,2},{7,3},{8,12},{9,13},{10,... | collective-permute-start | bytes 516104 | tf_op jit(solution)/shard_map/ppermute | solution.py:35

commit v2 on v1

--- a/solution.py
+++ b/solution.py
@@ -9,30 +9,26 @@
 F32, BF16 = jnp.float32, jnp.bfloat16
 
 
-def first(core):
-    return 1 if core == 0 else 3
-
-
-def pairs(axis, step):
+def pairs(kind, off):
     out = []
     for g in range(8):
         z, c = divmod(g, 2)
-        off = first(c) if step == 0 else 4 - first(c)
         for e in range(16):
             y, x = divmod(e, 4)
-            x2 = x ^ off if axis == "x" else x
-            y2 = y ^ off if axis == "y" else y
-            z2 = z ^ off if axis == "z" else z
-            out.append((g * 16 + e, (2 * z2 + c) * 16 + 4 * y2 + x2))
+            place = {"x": x, "y": y, "z": z}
+            axis = {"z": "z", "in": "xy"[c], "out": "yx"[c]}[kind]
+            place[axis] ^= 4 - off if kind == "z" and c == 1 else off
+            out.append((g * 16 + e, (2 * place["z"] + c) * 16 + 4 * place["y"] + place["x"]))
     return out
 
 
-PAIRS = {axis: (pairs(axis, 0), pairs(axis, 1)) for axis in "xyz"}
+P_OFF, Q_OFF = 1, 3
+PAIRS = {(kind, off): pairs(kind, off) for kind in ("z", "in", "out") for off in (P_OFF, Q_OFF)}
 SWAP = [(g * 16 + e, (g ^ 1) * 16 + e) for g in range(8) for e in range(16)]
 
 
-def exchange(value, axis, step):
-    return lax.ppermute(value, BOTH, PAIRS[axis][step])
+def exchange(value, kind, off):
+    return lax.ppermute(value, BOTH, PAIRS[kind, off])
 
 
 def swap(value):
@@ -43,8 +39,7 @@
     table = []
     for g in range(8):
         z, c = divmod(g, 2)
-        p = first(c)
-        q = 4 - p
+        p, q = (P_OFF, Q_OFF) if c == 0 else (Q_OFF, P_OFF)
         own = [2 * (z ^ o) + c for o in (0, p, q, 2)]
         other = [2 * (z ^ o) + 1 - c for o in (0, q, p, 2)]
         table.append(own[:2] + other[:2] + own[2:] + other[2:])
@@ -100,70 +95,73 @@
     )(order, routed_slots.reshape(1, cap), combine.reshape(cap, 1), *flat)
 
 
-def gather_rows(own, axes):
-    value = own
-    for axis in axes:
-        for step in (0, 1):
-            got = exchange(value, axis, step)
-            if axis == axes[1] and step == 1:
-                return value, got
-            value = jnp.concatenate([value, got], axis=0)
-
-
 def dot(a, b):
     return jnp.dot(a, b, preferred_element_type=F32)
 
 
-def sum_rows(near, far, axes):
-    got = exchange(far, axes[0], 1)
-    rest = near
-    for axis, step in ((axes[0], 0), (axes[1], 1), (axes[1], 0)):
-        total = rest + got.astype(F32)
-        half = total.shape[0] // 2
-        rest = total[:half]
-        got = exchange(total[half:].astype(BF16), axis, step)
-    return rest, got
+def stack(*parts):
+    return jnp.concatenate(parts, axis=0)
+
+
+def together(*values):
+    return lax.optimization_barrier(values)
+
+
+def swap_parts(value, parts):
+    rows = value.shape[0] // parts
+    return stack(*(swap(value[i * rows : (i + 1) * rows]) for i in range(parts))) if parts > 1 else swap(value)
 
 
 def on_device(tokens, routed_slots, combine_weight, gate_weight, up_weight, down_weight):
-    cap = routed_slots.shape[0]
     order = jnp.asarray(shard_order(), jnp.int32)[lax.axis_index("grp")]
-
-    both = jnp.concatenate([gate_weight, up_weight], axis=1)
-    near_w = jnp.concatenate([both, exchange(both, "z", 0)], axis=0)
-    far_w = exchange(near_w, "z", 1)
-    near_w2, far_w2 = swap(near_w), swap(far_w)
+    cap, ff = routed_slots.shape[0], gate_weight.shape[1]
+    group = 4 * cap
+    p, q = P_OFF, Q_OFF
 
     own_a, own_b = pack(order, routed_slots, tokens)
-    near_a, far_a = gather_rows(own_a, "xy")
-    near_b, far_b = gather_rows(own_b, "yx")
+    a_1 = stack(own_a, exchange(own_a, "in", p))
+    b_1 = stack(own_b, exchange(own_b, "in", q))
+    w_0 = jnp.concatenate([gate_weight, up_weight], axis=1)
+    near_w = stack(w_0, exchange(w_0, "z", p))
+    a_2, b_2 = exchange(a_1, "in", q), exchange(b_1, "in", p)
+    a0 = stack(a_1, a_2)
+    b0 = stack(own_b, b_2[:cap], b_1[cap:], b_2[cap:])
 
-    near_d = jnp.concatenate([down_weight, exchange(down_weight, "z", 0)], axis=1)
-    far_d = exchange(near_d, "z", 1)
-    near_d2, far_d2 = swap(near_d), swap(far_d)
+    ap, bq = exchange(a0, "out", p), exchange(b0, "out", q)
+    near_a, near_b = stack(a0, ap), stack(b0, bq)
+    far_a, far_b = exchange(near_a, "out", q), exchange(near_b, "out", p)
+    far_w = exchange(near_w, "z", q)
+    near_w2, far_w2 = swap_parts(near_w, 1), swap_parts(far_w, 1)
+    near_d = jnp.concatenate([down_weight, exchange(down_weight, "z", p)], axis=1)
+    far_d = exchange(near_d, "z", q)
+    near_d2, far_d2 = swap_parts(near_d, 1), swap_parts(far_d, 1)
 
     k = near_w.shape[0]
+    act = lambda acc: (jax.nn.silu(acc[:, :ff]) * acc[:, ff:]).astype(BF16)
+    acc_near_a = dot(near_a[:, :k], near_w) + dot(near_a[:, k:], near_w2)
+    acc_near_b = dot(near_b[:, :k], far_w)
+    far_a, far_b, acc_near_a, acc_near_b = together(far_a, far_b, acc_near_a, acc_near_b)
+    acc_near_b = acc_near_b + dot(near_b[:, k:], far_w2)
+    acc_far_a = dot(far_a[:, :k], near_w) + dot(far_a[:, k:], near_w2)
+    acc_far_b = dot(far_b[:, :k], far_w) + dot(far_b[:, k:], far_w2)
+    h_q2 = act(acc_far_a + stack(acc_near_b[group:], acc_far_b[group:]))
+    h_0p = act(acc_near_a + stack(acc_near_b[:group], acc_far_b[:group]))
+    h_p2 = stack(h_0p[group:], h_q2[group:])
+    h_0q = stack(h_0p[:group], h_q2[:group])
 
-    def up_sums(rows, w, w2):
-        return dot(rows[:, :k], w) + dot(rows[:, k:], w2)
 
-    acc_a = jnp.concatenate([up_sums(near_a, near_w, near_w2), up_sums(far_a, near_w, near_w2)], axis=0)
-    acc_b = jnp.concatenate([up_sums(near_b, far_w, far_w2), up_sums(far_b, far_w, far_w2)], axis=0)
-    wide = acc_a.shape[1]
-
-    def other_order(v):
-        return v.reshape(4, 4, cap, -1).swapaxes(0, 1).reshape(16 * cap, -1)
-
-    acc = acc_a + other_order(acc_b)
-    ff = wide // 2
-    hidden_a = (jax.nn.silu(acc[:, :ff]) * acc[:, ff:]).astype(BF16)
-    hidden_b = other_order(hidden_a)
-
-    half = 8 * cap
     pieces = []
-    for w, w2 in ((near_d, near_d2), (far_d, far_d2)):
-        for h, wd, axes in ((hidden_a, w, "yx"), (hidden_b, w2, "xy")):
-            pieces.append(sum_rows(dot(h[:half], wd), dot(h[half:], wd).astype(BF16), axes))
+    for wds in ((near_d, near_d2), (far_d, far_d2)):
+        for stay, leave, wd, off in ((h_0p, h_q2, wds[0], q), (h_0q, h_p2, wds[1], p)):
+            got = exchange(dot(leave, wd).astype(BF16), "out", off)
+            total = dot(stay, wd) + got.astype(F32)
+            got = exchange(total[group:].astype(BF16), "out", 4 - off)
+            total = total[:group] + got.astype(F32)
+            block = lambda i: total[i * cap : (i + 1) * cap]
+            one, two = (block(1), block(2)) if off == p else (block(2), block(1))
+            got = exchange(stack(one, block(3)).astype(BF16), "in", off).astype(F32)
+            last = exchange((two + got[cap:]).astype(BF16), "in", 4 - off)
+            pieces.append((block(0) + got[:cap], last))
     return place(order, routed_slots, combine_weight, pieces, tokens.shape[0])
 
 

time: 185 us -> 173 us (0.935); the launches traced: 182 us -> 173 us
  waiting for transfers between devices: 106 us -> 94.9 us
  starting transfers between devices: 41.1 us -> 47 us
  local copies, waits for them, and re-layouts: 7.43 us -> 4.52 us
    ppermute x28, waiting for transfers between devices: 106 us -> 94.9 us  [exchange(): return lax.ppermute(value, BOTH, PAIRS[kind, off])]
    ppermute x28, starting transfers between devices: 40.6 us -> 46.4 us  [exchange(): return lax.ppermute(value, BOTH, PAIRS[kind, off])]
    slice x17 -> x10, local copies, waits for them, and re-layouts: 3.37 us -> 0.95 us  [the longest x1 0.45 us: on_device(): h_q2 = act(acc_far_a + stack(acc_near_b[group:], acc_far_b[group:]))]
  transfers between devices with their start and end apart: 32 -> 32, of which waited for: 18 -> 15; matrix products, arithmetic and copies ran while one was open for 16% -> 14% of each run, Pallas kernels for 0% -> 0%
where the time goes in v2:
time: 173 us
  waiting for transfers between devices  94.9 us (55%)
  starting transfers between devices  47 us (27%)
  matrix products  19.9 us (12%)
  local copies, waits for them, and re-layouts  4.52 us (3%)
  Pallas kernels  3.29 us (2%)
  other arithmetic  2.88 us (2%)
    ppermute x28, waiting for transfers between devices, exchange(): return lax.ppermute(value, BOTH, PAIRS[kind, off])  94.9 us
    ppermute x28, starting transfers between devices, exchange(): return lax.ppermute(value, BOTH, PAIRS[kind, off])  46.4 us
    dot_general x16, matrix products, dot(): return jnp.dot(a, b, preferred_element_type=F32)  19.9 us
  transfers between devices with their start and end apart: 32, of which 15 were waited for; matrix products, arithmetic and copies ran while one was open for 14% of the time, Pallas kernels for 0%

profile of v2, /device:TPU:0, one launch (start us, length us, event | category | flops | bytes accessed | tf_op | source)
XLA Modules:
  0.0 173.0 jit_solution(11005481265483743475)
XLA Ops:
  0.0 0.7 dynamic-slice_bitcast_fusion.order_ref
  0.7 1.4 copy-done
  2.1 0.7 copy-done.1
  2.8 1.0 pack.1
  3.7 1.7 collective-permute-start
  5.6 2.0 %collective-permute-start.8 = (bf16[768,1024]{1,0:T(8,128)(2,1)S(1)}, bf16[768,1024]{1,0:T(8,128)(2,1)S(1)}, u32[]{:S(2)}, u32[]{:S(2)}) collective-permute-start(bf16[768,1024]{1,0:T(8,128)(2,1)S(1)} %constant_dynamic-update-slice_fusion.9), channel_id=1, source_target_pairs={{0,32},{1,33},{2,34},{3,35},{4,36},{5,37},{6,38},{7,39},{8,40},{9,... | collective-permute-start | bytes 4718600 | tf_op jit(solution)/shard_map/ppermute | solution.py:31
  7.6 2.1 %collective-permute-start.4 = (bf16[56,3072]{1,0:T(8,128)(2,1)S(1)}, bf16[56,3072]{1,0:T(8,128)(2,1)S(1)}, u32[]{:S(2)}, u32[]{:S(2)}) collective-permute-start(bf16[56,3072]{1,0:T(8,128)(2,1)S(1)} %get-tuple-element.12), channel_id=1, source_target_pairs={{0,3},{1,2},{2,1},{3,0},{4,7},{5,6},{6,5},{7,4},{8,11},{9,10},{10,... | collective-permute-start | bytes 1032200 | tf_op jit(solution)/shard_map/ppermute | solution.py:31
  9.9 1.2 collective-permute-done
  11.1 2.9 %collective-permute-start.1 = (bf16[112,3072]{1,0:T(8,128)(2,1)S(1)}, bf16[112,3072]{1,0:T(8,128)(2,1)S(1)}, u32[]{:S(2)}, u32[]{:S(2)}) collective-permute-start(bf16[112,3072]{1,0:T(8,128)(2,1)S(1)} %pad_maximum_fusion.3), channel_id=1, source_target_pairs={{0,3},{1,2},{2,1},{3,0},{4,7},{5,6},{6,5},{7,4},{8,11},{9,10},{10,... | collective-permute-start | bytes 2064392 | tf_op jit(solution)/shard_map/ppermute | solution.py:31
  14.0 2.0 %collective-permute-done.4 = bf16[56,3072]{1,0:T(8,128)(2,1)S(1)} collective-permute-done((bf16[56,3072]{1,0:T(8,128)(2,1)S(1)}, bf16[56,3072]{1,0:T(8,128)(2,1)S(1)}, u32[]{:S(2)}, u32[]{:S(2)}) %collective-permute-start.4) | collective-permute-done | bytes 344096 | tf_op jit(solution)/shard_map/ppermute | solution.py:31
  16.2 7.2 %collective-permute-done.1 = bf16[112,3072]{1,0:T(8,128)(2,1)S(1)} collective-permute-done((bf16[112,3072]{1,0:T(8,128)(2,1)S(1)}, bf16[112,3072]{1,0:T(8,128)(2,1)S(1)}, u32[]{:S(2)}, u32[]{:S(2)}) %collective-permute-start.1) | collective-permute-done | bytes 688160 | tf_op jit(solution)/shard_map/ppermute | solution.py:31
  23.5 1.7 collective-permute-start.2
  25.2 0.9 collective-permute-done.8
  26.4 4.1 %collective-permute-start.10 = (bf16[1536,1024]{1,0:T(8,128)(2,1)S(1)}, bf16[1536,1024]{1,0:T(8,128)(2,1)S(1)}, u32[]{:S(2)}, u32[]{:S(2)}) collective-permute-start(bf16[1536,1024]{1,0:T(8,128)(2,1)S(1)} %pad_maximum_fusion), channel_id=1, source_target_pairs={{0,96},{1,97},{2,98},{3,99},{4,100},{5,101},{6,102},{7,103},{8,104... | collective-permute-start | bytes 9437192 | tf_op jit(solution)/shard_map/ppermute | solution.py:31
  30.7 3.1 %collective-permute-start.6 = (bf16[224,3072]{1,0:T(8,128)(2,1)S(1)}, bf16[224,3072]{1,0:T(8,128)(2,1)S(1)}, u32[]{:S(2)}, u32[]{:S(2)}) collective-permute-start(bf16[224,3072]{1,0:T(8,128)(2,1)S(1)} %pad_maximum_fusion.2), channel_id=1, source_target_pairs={{0,12},{1,13},{2,14},{3,15},{4,8},{5,9},{6,10},{7,11},{8,4},{9,5},... | collective-permute-start | bytes 4128776 | tf_op jit(solution)/shard_map/ppermute | solution.py:31
  34.0 16.3 %collective-permute-done.6 = bf16[224,3072]{1,0:T(8,128)(2,1)S(1)} collective-permute-done((bf16[224,3072]{1,0:T(8,128)(2,1)S(1)}, bf16[224,3072]{1,0:T(8,128)(2,1)S(1)}, u32[]{:S(2)}, u32[]{:S(2)}) %collective-permute-start.6) | collective-permute-done | bytes 1376288 | tf_op jit(solution)/shard_map/ppermute | solution.py:31
  50.4 0.4 collective-permute-start.7
  51.0 2.8 %collective-permute-start.3 = (bf16[448,3072]{1,0:T(8,128)(2,1)S(1)}, bf16[448,3072]{1,0:T(8,128)(2,1)S(1)}, u32[]{:S(2)}, u32[]{:S(2)}) collective-permute-start(bf16[448,3072]{1,0:T(8,128)(2,1)S(1)} %constant_dynamic-update-slice_fusion), channel_id=1, source_target_pairs={{0,12},{1,13},{2,14},{3,15},{4,8},{5,9},{6,10},{7,11},{8,4},{9,5},... | collective-permute-start | bytes 8257544 | tf_op jit(solution)/shard_map/ppermute | solution.py:31
  53.9 1.1 collective-permute-start.22
  55.0 14.2 %collective-permute-done.10 = bf16[1536,1024]{1,0:T(8,128)(2,1)S(1)} collective-permute-done((bf16[1536,1024]{1,0:T(8,128)(2,1)S(1)}, bf16[1536,1024]{1,0:T(8,128)(2,1)S(1)}, u32[]{:S(2)}, u32[]{:S(2)}) %collective-permute-start.10) | collective-permute-done | bytes 3145760 | tf_op jit(solution)/shard_map/ppermute | solution.py:31
  69.2 1.6 fusion.1
  70.8 15.2 %collective-permute-done.22 = bf16[512,1536]{1,0:T(8,128)(2,1)S(1)} collective-permute-done((bf16[512,1536]{1,0:T(8,128)(2,1)S(1)}, bf16[512,1536]{1,0:T(8,128)(2,1)S(1)}, u32[]{:S(2)}, u32[]{:S(2)}) %collective-permute-start.22) | collective-permute-done | bytes 1572896 | tf_op jit(solution)/shard_map/ppermute | solution.py:31
  86.1 0.5 collective-permute-start.27
  86.6 1.6 fusion.3
  88.2 1.6 convolution_add_fusion.6
  89.8 1.6 fusion.6
  91.4 1.6 fusion.10
  93.0 1.6 convolution_add_fusion.4
  94.7 1.6 convolution_add_fusion.5
  96.3 0.4 fusion.24
  96.7 1.6 maximum_add_fusion.1
  98.7 0.3 maximum_add_fusion
  99.3 0.9 convolution_convert_fusion
  100.2 0.6 collective-permute-start.28
  100.8 0.9 convolution_convert_fusion.1
  101.7 3.1 %collective-permute-start.23 = (bf16[448,1536]{1,0:T(8,128)(2,1)S(1)}, bf16[448,1536]{1,0:T(8,128)(2,1)S(1)}, u32[]{:S(2)}, u32[]{:S(2)}) collective-permute-start(bf16[448,1536]{1,0:T(8,128)(2,1)S(1)} %convolution_convert_fusion.1), channel_id=1, source_target_pairs={{0,12},{1,13},{2,14},{3,15},{4,8},{5,9},{6,10},{7,11},{8,4},{9,5},... | collective-permute-start | bytes 4128776 | tf_op jit(solution)/shard_map/ppermute | solution.py:31
  104.7 0.9 convolution_convert_fusion.2
  105.6 0.4 collective-permute-start.18
  106.1 0.9 convolution_convert_fusion.3
  106.9 1.1 collective-permute-start.13
  108.1 10.5 %collective-permute-done.28 = bf16[448,1536]{1,0:T(8,128)(2,1)S(1)} collective-permute-done((bf16[448,1536]{1,0:T(8,128)(2,1)S(1)}, bf16[448,1536]{1,0:T(8,128)(2,1)S(1)}, u32[]{:S(2)}, u32[]{:S(2)}) %collective-permute-start.28) | collective-permute-done | bytes 1376288 | tf_op jit(solution)/shard_map/ppermute | solution.py:31
  118.6 0.9 convolution_add_fusion
  119.6 2.3 %collective-permute-start.29 = (bf16[224,1536]{1,0:T(8,128)(2,1)S(1)}, bf16[224,1536]{1,0:T(8,128)(2,1)S(1)}, u32[]{:S(2)}, u32[]{:S(2)}) collective-permute-start(bf16[224,1536]{1,0:T(8,128)(2,1)S(1)} %slice.320), channel_id=1, source_target_pairs={{0,12},{1,13},{2,14},{3,15},{4,8},{5,9},{6,10},{7,11},{8,4},{9,5},... | collective-permute-start | bytes 2064392 | tf_op jit(solution)/shard_map/ppermute | solution.py:31
  121.8 0.9 convolution_add_fusion.1
  122.8 0.8 collective-permute-start.24
  123.6 9.8 %collective-permute-done.18 = bf16[448,1536]{1,0:T(8,128)(2,1)S(1)} collective-permute-done((bf16[448,1536]{1,0:T(8,128)(2,1)S(1)}, bf16[448,1536]{1,0:T(8,128)(2,1)S(1)}, u32[]{:S(2)}, u32[]{:S(2)}) %collective-permute-start.18) | collective-permute-done | bytes 1376288 | tf_op jit(solution)/shard_map/ppermute | solution.py:31
  133.4 0.9 convolution_add_fusion.2
  134.3 2.3 %collective-permute-start.19 = (bf16[224,1536]{1,0:T(8,128)(2,1)S(1)}, bf16[224,1536]{1,0:T(8,128)(2,1)S(1)}, u32[]{:S(2)}, u32[]{:S(2)}) collective-permute-start(bf16[224,1536]{1,0:T(8,128)(2,1)S(1)} %slice.322), channel_id=1, source_target_pairs={{0,12},{1,13},{2,14},{3,15},{4,8},{5,9},{6,10},{7,11},{8,4},{9,5},... | collective-permute-start | bytes 2064392 | tf_op jit(solution)/shard_map/ppermute | solution.py:31
  136.6 0.9 convolution_add_fusion.3
  137.6 0.8 collective-permute-start.14
  138.3 5.1 %collective-permute-done.29 = bf16[224,1536]{1,0:T(8,128)(2,1)S(1)} collective-permute-done((bf16[224,1536]{1,0:T(8,128)(2,1)S(1)}, bf16[224,1536]{1,0:T(8,128)(2,1)S(1)}, u32[]{:S(2)}, u32[]{:S(2)}) %collective-permute-start.29) | collective-permute-done | bytes 688160 | tf_op jit(solution)/shard_map/ppermute | solution.py:31
  143.7 1.6 collective-permute-start.30
  145.5 2.2 %collective-permute-start.25 = (bf16[112,1536]{1,0:T(8,128)(2,1)S(1)}, bf16[112,1536]{1,0:T(8,128)(2,1)S(1)}, u32[]{:S(2)}, u32[]{:S(2)}) collective-permute-start(bf16[112,1536]{1,0:T(8,128)(2,1)S(1)} %concatenate.77), channel_id=1, source_target_pairs={{0,3},{1,2},{2,1},{3,0},{4,7},{5,6},{6,5},{7,4},{8,11},{9,10},{10,... | collective-permute-start | bytes 1032200 | tf_op jit(solution)/shard_map/ppermute | solution.py:31
  147.6 6.1 %collective-permute-done.19 = bf16[224,1536]{1,0:T(8,128)(2,1)S(1)} collective-permute-done((bf16[224,1536]{1,0:T(8,128)(2,1)S(1)}, bf16[224,1536]{1,0:T(8,128)(2,1)S(1)}, u32[]{:S(2)}, u32[]{:S(2)}) %collective-permute-start.19) | collective-permute-done | bytes 688160 | tf_op jit(solution)/shard_map/ppermute | solution.py:31
  154.0 2.3 %collective-permute-start.20 = (bf16[112,1536]{1,0:T(8,128)(2,1)S(1)}, bf16[112,1536]{1,0:T(8,128)(2,1)S(1)}, u32[]{:S(2)}, u32[]{:S(2)}) collective-permute-start(bf16[112,1536]{1,0:T(8,128)(2,1)S(1)} %pad_maximum_fusion.7), channel_id=1, source_target_pairs={{0,1},{1,0},{2,3},{3,2},{4,5},{5,4},{6,7},{7,6},{8,9},{9,8},{10,11... | collective-permute-start | bytes 1032200 | tf_op jit(solution)/shard_map/ppermute | solution.py:31
  156.5 2.2 %collective-permute-start.15 = (bf16[112,1536]{1,0:T(8,128)(2,1)S(1)}, bf16[112,1536]{1,0:T(8,128)(2,1)S(1)}, u32[]{:S(2)}, u32[]{:S(2)}) collective-permute-start(bf16[112,1536]{1,0:T(8,128)(2,1)S(1)} %concatenate.78), channel_id=1, source_target_pairs={{0,3},{1,2},{2,1},{3,0},{4,7},{5,6},{6,5},{7,4},{8,11},{9,10},{10,... | collective-permute-start | bytes 1032200 | tf_op jit(solution)/shard_map/ppermute | solution.py:31
  158.9 1.2 collective-permute-start.31
  160.3 1.2 collective-permute-done.20
  161.7 3.3 %collective-permute-start.21 = (bf16[56,1536]{1,0:T(8,128)(2,1)S(1)}, bf16[56,1536]{1,0:T(8,128)(2,1)S(1)}, u32[]{:S(2)}, u32[]{:S(2)}) collective-permute-start(bf16[56,1536]{1,0:T(8,128)(2,1)S(1)} %get-tuple-element.25), channel_id=1, source_target_pairs={{0,3},{1,2},{2,1},{3,0},{4,7},{5,6},{6,5},{7,4},{8,11},{9,10},{10,... | collective-permute-start | bytes 516104 | tf_op jit(solution)/shard_map/ppermute | solution.py:31
  165.2 0.3 collective-permute-start.16
  165.7 1.2 collective-permute-done.31.refs_7_
  166.9 1.8 %collective-permute-done.21.refs_3_ = bf16[56,1536]{1,0:T(8,128)(2,1)S(1)} collective-permute-done((bf16[56,1536]{1,0:T(8,128)(2,1)S(1)}, bf16[56,1536]{1,0:T(8,128)(2,1)S(1)}, u32[]{:S(2)}, u32[]{:S(2)}) %collective-permute-start.21) | collective-permute-done | bytes 172064 | tf_op jit(solution)/shard_map/ppermute | solution.py:31
  168.7 2.0 %collective-permute-done.16.refs_1_ = bf16[56,1536]{1,0:T(8,128)(2,1)S(1)} collective-permute-done((bf16[56,1536]{1,0:T(8,128)(2,1)S(1)}, bf16[56,1536]{1,0:T(8,128)(2,1)S(1)}, u32[]{:S(2)}, u32[]{:S(2)}) %collective-permute-start.16) | collective-permute-done | bytes 172064 | tf_op jit(solution)/shard_map/ppermute | solution.py:31
  170.7 2.3 %place.1 = bf16[128,6144]{1,0:T(8,128)(2,1)} custom-call(s32[8]{0:T(128)S(1)} %dynamic-slice_bitcast_fusion.order_ref, s32[1,56]{1,0:T(1,128)S(1)} %bitcast.23, f32[56,1]{1,0:T(8,128)S(1)} %copy.8.combine_ref, f32[56,1536]{1,0:T(8,128)S(1)} %get-tuple-element.28.refs_0_, bf16[56,1536]{1,0:T(8,128)(2,1)S(1)} %collective-permute-done.16.refs_1_, ...), custom_call_target="tpu_custom_call" | custom-call | tf_op jit(solution)/shard_map/place/pallas_call | solution.py:88
  (80 shorter events, 4.3 us)
Async XLA Ops:
  0.7 1.4 copy-start
  2.1 0.7 copy-start.1
  2.8 2.6 %copy-start.3 = (bf16[768,512]{1,0:T(8,128)(2,1)S(1)}, bf16[768,512]{1,0:T(8,128)(2,1)}, u32[]{:S(2)}) copy-start(bf16[768,512]{1,0:T(8,128)(2,1)} %param.10) | copy-start | bytes 2359300
  2.8 2.7 %copy-start.4 = (bf16[768,512]{1,0:T(8,128)(2,1)S(1)}, bf16[768,512]{1,0:T(8,128)(2,1)}, u32[]{:S(2)}) copy-start(bf16[768,512]{1,0:T(8,128)(2,1)} %param.11) | copy-start | bytes 2359300
  3.7 6.0 %copy-start.5 = (bf16[512,768]{1,0:T(8,128)(2,1)S(1)}, bf16[512,768]{1,0:T(8,128)(2,1)}, u32[]{:S(2)}) copy-start(bf16[512,768]{1,0:T(8,128)(2,1)} %param.12) | copy-start | bytes 2359300
  3.7 7.3 %collective-permute-start = (bf16[56,3072]{1,0:T(8,128)(2,1)S(1)}, bf16[56,3072]{1,0:T(8,128)(2,1)S(1)}, u32[]{:S(2)}, u32[]{:S(2)}) collective-permute-start(bf16[56,3072]{1,0:T(8,128)(2,1)S(1)} %get-tuple-element.11), channel_id=1, source_target_pairs={{0,1},{1,0},{2,3},{3,2},{4,5},{5,4},{6,7},{7,6},{8,9},{9,8},{10,11... | collective-permute-start | bytes 1032200 | tf_op jit(solution)/shard_map/ppermute | solution.py:31
  5.6 20.5 %collective-permute-start.8 = (bf16[768,1024]{1,0:T(8,128)(2,1)S(1)}, bf16[768,1024]{1,0:T(8,128)(2,1)S(1)}, u32[]{:S(2)}, u32[]{:S(2)}) collective-permute-start(bf16[768,1024]{1,0:T(8,128)(2,1)S(1)} %constant_dynamic-update-slice_fusion.9), channel_id=1, source_target_pairs={{0,32},{1,33},{2,34},{3,35},{4,36},{5,37},{6,38},{7,39},{8,40},{9,... | collective-permute-start | bytes 4718600 | tf_op jit(solution)/shard_map/ppermute | solution.py:31
  7.6 8.5 %collective-permute-start.4 = (bf16[56,3072]{1,0:T(8,128)(2,1)S(1)}, bf16[56,3072]{1,0:T(8,128)(2,1)S(1)}, u32[]{:S(2)}, u32[]{:S(2)}) collective-permute-start(bf16[56,3072]{1,0:T(8,128)(2,1)S(1)} %get-tuple-element.12), channel_id=1, source_target_pairs={{0,3},{1,2},{2,1},{3,0},{4,7},{5,6},{6,5},{7,4},{8,11},{9,10},{10,... | collective-permute-start | bytes 1032200 | tf_op jit(solution)/shard_map/ppermute | solution.py:31
  9.7 44.1 %collective-permute-start.12 = (bf16[512,768]{1,0:T(8,128)(2,1)S(1)}, bf16[512,768]{1,0:T(8,128)(2,1)S(1)}, u32[]{:S(2)}, u32[]{:S(2)}) collective-permute-start(bf16[512,768]{1,0:T(8,128)(2,1)S(1)} %copy-done.5), channel_id=1, source_target_pairs={{0,32},{1,33},{2,34},{3,35},{4,36},{5,37},{6,38},{7,39},{8,40},{9,... | collective-permute-start | bytes 2359304 | tf_op jit(solution)/shard_map/ppermute | solution.py:31
  11.1 12.3 %collective-permute-start.1 = (bf16[112,3072]{1,0:T(8,128)(2,1)S(1)}, bf16[112,3072]{1,0:T(8,128)(2,1)S(1)}, u32[]{:S(2)}, u32[]{:S(2)}) collective-permute-start(bf16[112,3072]{1,0:T(8,128)(2,1)S(1)} %pad_maximum_fusion.3), channel_id=1, source_target_pairs={{0,3},{1,2},{2,1},{3,0},{4,7},{5,6},{6,5},{7,4},{8,11},{9,10},{10,... | collective-permute-start | bytes 2064392 | tf_op jit(solution)/shard_map/ppermute | solution.py:31
  16.1 14.4 %collective-permute-start.5 = (bf16[112,3072]{1,0:T(8,128)(2,1)S(1)}, bf16[112,3072]{1,0:T(8,128)(2,1)S(1)}, u32[]{:S(2)}, u32[]{:S(2)}) collective-permute-start(bf16[112,3072]{1,0:T(8,128)(2,1)S(1)} %pad_maximum_fusion.4), channel_id=1, source_target_pairs={{0,1},{1,0},{2,3},{3,2},{4,5},{5,4},{6,7},{7,6},{8,9},{9,8},{10,11... | collective-permute-start | bytes 2064392 | tf_op jit(solution)/shard_map/ppermute | solution.py:31
  23.5 27.4 %collective-permute-start.2 = (bf16[224,3072]{1,0:T(8,128)(2,1)S(1)}, bf16[224,3072]{1,0:T(8,128)(2,1)S(1)}, u32[]{:S(2)}, u32[]{:S(2)}) collective-permute-start(bf16[224,3072]{1,0:T(8,128)(2,1)S(1)} %pad_maximum_fusion.1), channel_id=1, source_target_pairs={{0,4},{1,5},{2,6},{3,7},{4,0},{5,1},{6,2},{7,3},{8,12},{9,13},{10,... | collective-permute-start | bytes 4128776 | tf_op jit(solution)/shard_map/ppermute | solution.py:31
  26.4 42.8 %collective-permute-start.10 = (bf16[1536,1024]{1,0:T(8,128)(2,1)S(1)}, bf16[1536,1024]{1,0:T(8,128)(2,1)S(1)}, u32[]{:S(2)}, u32[]{:S(2)}) collective-permute-start(bf16[1536,1024]{1,0:T(8,128)(2,1)S(1)} %pad_maximum_fusion), channel_id=1, source_target_pairs={{0,96},{1,97},{2,98},{3,99},{4,100},{5,101},{6,102},{7,103},{8,104... | collective-permute-start | bytes 9437192 | tf_op jit(solution)/shard_map/ppermute | solution.py:31
  30.7 19.6 %collective-permute-start.6 = (bf16[224,3072]{1,0:T(8,128)(2,1)S(1)}, bf16[224,3072]{1,0:T(8,128)(2,1)S(1)}, u32[]{:S(2)}, u32[]{:S(2)}) collective-permute-start(bf16[224,3072]{1,0:T(8,128)(2,1)S(1)} %pad_maximum_fusion.2), channel_id=1, source_target_pairs={{0,12},{1,13},{2,14},{3,15},{4,8},{5,9},{6,10},{7,11},{8,4},{9,5},... | collective-permute-start | bytes 4128776 | tf_op jit(solution)/shard_map/ppermute | solution.py:31
  33.9 52.1 %collective-permute-start.9 = (bf16[1536,1024]{1,0:T(8,128)(2,1)S(1)}, bf16[1536,1024]{1,0:T(8,128)(2,1)S(1)}, u32[]{:S(2)}, u32[]{:S(2)}) collective-permute-start(bf16[1536,1024]{1,0:T(8,128)(2,1)S(1)} %pad_maximum_fusion), channel_id=1, source_target_pairs={{0,16},{1,17},{2,18},{3,19},{4,20},{5,21},{6,22},{7,23},{8,24},{9,... | collective-permute-start | bytes 9437192 | tf_op jit(solution)/shard_map/ppermute | solution.py:35
  50.4 39.4 %collective-permute-start.7 = (bf16[448,3072]{1,0:T(8,128)(2,1)S(1)}, bf16[448,3072]{1,0:T(8,128)(2,1)S(1)}, u32[]{:S(2)}, u32[]{:S(2)}) collective-permute-start(bf16[448,3072]{1,0:T(8,128)(2,1)S(1)} %constant_dynamic-update-slice_fusion.4), channel_id=1, source_target_pairs={{0,4},{1,5},{2,6},{3,7},{4,0},{5,1},{6,2},{7,3},{8,12},{9,13},{10,... | collective-permute-start | bytes 8257544 | tf_op jit(solution)/shard_map/ppermute | solution.py:31
  51.0 38.8 %collective-permute-start.3 = (bf16[448,3072]{1,0:T(8,128)(2,1)S(1)}, bf16[448,3072]{1,0:T(8,128)(2,1)S(1)}, u32[]{:S(2)}, u32[]{:S(2)}) collective-permute-start(bf16[448,3072]{1,0:T(8,128)(2,1)S(1)} %constant_dynamic-update-slice_fusion), channel_id=1, source_target_pairs={{0,12},{1,13},{2,14},{3,15},{4,8},{5,9},{6,10},{7,11},{8,4},{9,5},... | collective-permute-start | bytes 8257544 | tf_op jit(solution)/shard_map/ppermute | solution.py:31
  53.9 32.2 %collective-permute-start.22 = (bf16[512,1536]{1,0:T(8,128)(2,1)S(1)}, bf16[512,1536]{1,0:T(8,128)(2,1)S(1)}, u32[]{:S(2)}, u32[]{:S(2)}) collective-permute-start(bf16[512,1536]{1,0:T(8,128)(2,1)S(1)} %constant_dynamic-update-slice_fusion.11), channel_id=1, source_target_pairs={{0,96},{1,97},{2,98},{3,99},{4,100},{5,101},{6,102},{7,103},{8,104... | collective-permute-start | bytes 4718600 | tf_op jit(solution)/shard_map/ppermute | solution.py:31
  69.2 23.8 %collective-permute-start.11 = (bf16[1536,1024]{1,0:T(8,128)(2,1)S(1)}, bf16[1536,1024]{1,0:T(8,128)(2,1)S(1)}, u32[]{:S(2)}, u32[]{:S(2)}) collective-permute-start(bf16[1536,1024]{1,0:T(8,128)(2,1)S(1)} %collective-permute-done.10), channel_id=1, source_target_pairs={{0,16},{1,17},{2,18},{3,19},{4,20},{5,21},{6,22},{7,23},{8,24},{9,... | collective-permute-start | bytes 9437192 | tf_op jit(solution)/shard_map/ppermute | solution.py:35
  86.0 18.7 %collective-permute-start.17 = (bf16[512,1536]{1,0:T(8,128)(2,1)S(1)}, bf16[512,1536]{1,0:T(8,128)(2,1)S(1)}, u32[]{:S(2)}, u32[]{:S(2)}) collective-permute-start(bf16[512,1536]{1,0:T(8,128)(2,1)S(1)} %constant_dynamic-update-slice_fusion.11), channel_id=1, source_target_pairs={{0,16},{1,17},{2,18},{3,19},{4,20},{5,21},{6,22},{7,23},{8,24},{9,... | collective-permute-start | bytes 4718600 | tf_op jit(solution)/shard_map/ppermute | solution.py:35
  86.1 13.3 %collective-permute-start.27 = (bf16[512,1536]{1,0:T(8,128)(2,1)S(1)}, bf16[512,1536]{1,0:T(8,128)(2,1)S(1)}, u32[]{:S(2)}, u32[]{:S(2)}) collective-permute-start(bf16[512,1536]{1,0:T(8,128)(2,1)S(1)} %collective-permute-done.22), channel_id=1, source_target_pairs={{0,16},{1,17},{2,18},{3,19},{4,20},{5,21},{6,22},{7,23},{8,24},{9,... | collective-permute-start | bytes 4718600 | tf_op jit(solution)/shard_map/ppermute | solution.py:35
  100.2 18.4 %collective-permute-start.28 = (bf16[448,1536]{1,0:T(8,128)(2,1)S(1)}, bf16[448,1536]{1,0:T(8,128)(2,1)S(1)}, u32[]{:S(2)}, u32[]{:S(2)}) collective-permute-start(bf16[448,1536]{1,0:T(8,128)(2,1)S(1)} %convolution_convert_fusion), channel_id=1, source_target_pairs={{0,4},{1,5},{2,6},{3,7},{4,0},{5,1},{6,2},{7,3},{8,12},{9,13},{10,... | collective-permute-start | bytes 4128776 | tf_op jit(solution)/shard_map/ppermute | solution.py:31
  101.7 20.2 %collective-permute-start.23 = (bf16[448,1536]{1,0:T(8,128)(2,1)S(1)}, bf16[448,1536]{1,0:T(8,128)(2,1)S(1)}, u32[]{:S(2)}, u32[]{:S(2)}) collective-permute-start(bf16[448,1536]{1,0:T(8,128)(2,1)S(1)} %convolution_convert_fusion.1), channel_id=1, source_target_pairs={{0,12},{1,13},{2,14},{3,15},{4,8},{5,9},{6,10},{7,11},{8,4},{9,5},... | collective-permute-start | bytes 4128776 | tf_op jit(solution)/shard_map/ppermute | solution.py:31
  105.6 27.7 %collective-permute-start.18 = (bf16[448,1536]{1,0:T(8,128)(2,1)S(1)}, bf16[448,1536]{1,0:T(8,128)(2,1)S(1)}, u32[]{:S(2)}, u32[]{:S(2)}) collective-permute-start(bf16[448,1536]{1,0:T(8,128)(2,1)S(1)} %convolution_convert_fusion.2), channel_id=1, source_target_pairs={{0,4},{1,5},{2,6},{3,7},{4,0},{5,1},{6,2},{7,3},{8,12},{9,13},{10,... | collective-permute-start | bytes 4128776 | tf_op jit(solution)/shard_map/ppermute | solution.py:31
  106.9 29.6 %collective-permute-start.13 = (bf16[448,1536]{1,0:T(8,128)(2,1)S(1)}, bf16[448,1536]{1,0:T(8,128)(2,1)S(1)}, u32[]{:S(2)}, u32[]{:S(2)}) collective-permute-start(bf16[448,1536]{1,0:T(8,128)(2,1)S(1)} %convolution_convert_fusion.3), channel_id=1, source_target_pairs={{0,12},{1,13},{2,14},{3,15},{4,8},{5,9},{6,10},{7,11},{8,4},{9,5},... | collective-permute-start | bytes 4128776 | tf_op jit(solution)/shard_map/ppermute | solution.py:31
  119.6 23.8 %collective-permute-start.29 = (bf16[224,1536]{1,0:T(8,128)(2,1)S(1)}, bf16[224,1536]{1,0:T(8,128)(2,1)S(1)}, u32[]{:S(2)}, u32[]{:S(2)}) collective-permute-start(bf16[224,1536]{1,0:T(8,128)(2,1)S(1)} %slice.320), channel_id=1, source_target_pairs={{0,12},{1,13},{2,14},{3,15},{4,8},{5,9},{6,10},{7,11},{8,4},{9,5},... | collective-permute-start | bytes 2064392 | tf_op jit(solution)/shard_map/ppermute | solution.py:31
  122.8 22.4 %collective-permute-start.24 = (bf16[224,1536]{1,0:T(8,128)(2,1)S(1)}, bf16[224,1536]{1,0:T(8,128)(2,1)S(1)}, u32[]{:S(2)}, u32[]{:S(2)}) collective-permute-start(bf16[224,1536]{1,0:T(8,128)(2,1)S(1)} %slice.321), channel_id=1, source_target_pairs={{0,4},{1,5},{2,6},{3,7},{4,0},{5,1},{6,2},{7,3},{8,12},{9,13},{10,... | collective-permute-start | bytes 2064392 | tf_op jit(solution)/shard_map/ppermute | solution.py:31
  134.3 19.4 %collective-permute-start.19 = (bf16[224,1536]{1,0:T(8,128)(2,1)S(1)}, bf16[224,1536]{1,0:T(8,128)(2,1)S(1)}, u32[]{:S(2)}, u32[]{:S(2)}) collective-permute-start(bf16[224,1536]{1,0:T(8,128)(2,1)S(1)} %slice.322), channel_id=1, source_target_pairs={{0,12},{1,13},{2,14},{3,15},{4,8},{5,9},{6,10},{7,11},{8,4},{9,5},... | collective-permute-start | bytes 2064392 | tf_op jit(solution)/shard_map/ppermute | solution.py:31
  137.6 18.8 %collective-permute-start.14 = (bf16[224,1536]{1,0:T(8,128)(2,1)S(1)}, bf16[224,1536]{1,0:T(8,128)(2,1)S(1)}, u32[]{:S(2)}, u32[]{:S(2)}) collective-permute-start(bf16[224,1536]{1,0:T(8,128)(2,1)S(1)} %slice.323), channel_id=1, source_target_pairs={{0,4},{1,5},{2,6},{3,7},{4,0},{5,1},{6,2},{7,3},{8,12},{9,13},{10,... | collective-permute-start | bytes 2064392 | tf_op jit(solution)/shard_map/ppermute | solution.py:31
  143.7 15.0 %collective-permute-start.30 = (bf16[112,1536]{1,0:T(8,128)(2,1)S(1)}, bf16[112,1536]{1,0:T(8,128)(2,1)S(1)}, u32[]{:S(2)}, u32[]{:S(2)}) collective-permute-start(bf16[112,1536]{1,0:T(8,128)(2,1)S(1)} %pad_maximum_fusion.8), channel_id=1, source_target_pairs={{0,1},{1,0},{2,3},{3,2},{4,5},{5,4},{6,7},{7,6},{8,9},{9,8},{10,11... | collective-permute-start | bytes 1032200 | tf_op jit(solution)/shard_map/ppermute | solution.py:31
  145.5 14.6 %collective-permute-start.25 = (bf16[112,1536]{1,0:T(8,128)(2,1)S(1)}, bf16[112,1536]{1,0:T(8,128)(2,1)S(1)}, u32[]{:S(2)}, u32[]{:S(2)}) collective-permute-start(bf16[112,1536]{1,0:T(8,128)(2,1)S(1)} %concatenate.77), channel_id=1, source_target_pairs={{0,3},{1,2},{2,1},{3,0},{4,7},{5,6},{6,5},{7,4},{8,11},{9,10},{10,... | collective-permute-start | bytes 1032200 | tf_op jit(solution)/shard_map/ppermute | solution.py:31
  154.0 7.5 %collective-permute-start.20 = (bf16[112,1536]{1,0:T(8,128)(2,1)S(1)}, bf16[112,1536]{1,0:T(8,128)(2,1)S(1)}, u32[]{:S(2)}, u32[]{:S(2)}) collective-permute-start(bf16[112,1536]{1,0:T(8,128)(2,1)S(1)} %pad_maximum_fusion.7), channel_id=1, source_target_pairs={{0,1},{1,0},{2,3},{3,2},{4,5},{5,4},{6,7},{7,6},{8,9},{9,8},{10,11... | collective-permute-start | bytes 1032200 | tf_op jit(solution)/shard_map/ppermute | solution.py:31
  156.5 8.5 %collective-permute-start.15 = (bf16[112,1536]{1,0:T(8,128)(2,1)S(1)}, bf16[112,1536]{1,0:T(8,128)(2,1)S(1)}, u32[]{:S(2)}, u32[]{:S(2)}) collective-permute-start(bf16[112,1536]{1,0:T(8,128)(2,1)S(1)} %concatenate.78), channel_id=1, source_target_pairs={{0,3},{1,2},{2,1},{3,0},{4,7},{5,6},{6,5},{7,4},{8,11},{9,10},{10,... | collective-permute-start | bytes 1032200 | tf_op jit(solution)/shard_map/ppermute | solution.py:31
  158.9 8.0 %collective-permute-start.31 = (bf16[56,1536]{1,0:T(8,128)(2,1)S(1)}, bf16[56,1536]{1,0:T(8,128)(2,1)S(1)}, u32[]{:S(2)}, u32[]{:S(2)}) collective-permute-start(bf16[56,1536]{1,0:T(8,128)(2,1)S(1)} %get-tuple-element.21), channel_id=1, source_target_pairs={{0,3},{1,2},{2,1},{3,0},{4,7},{5,6},{6,5},{7,4},{8,11},{9,10},{10,... | collective-permute-start | bytes 516104 | tf_op jit(solution)/shard_map/ppermute | solution.py:31
  160.3 6.7 %collective-permute-start.26 = (bf16[56,1536]{1,0:T(8,128)(2,1)S(1)}, bf16[56,1536]{1,0:T(8,128)(2,1)S(1)}, u32[]{:S(2)}, u32[]{:S(2)}) collective-permute-start(bf16[56,1536]{1,0:T(8,128)(2,1)S(1)} %get-tuple-element.23), channel_id=1, source_target_pairs={{0,1},{1,0},{2,3},{3,2},{4,5},{5,4},{6,7},{7,6},{8,9},{9,8},{10,11... | collective-permute-start | bytes 516104 | tf_op jit(solution)/shard_map/ppermute | solution.py:31
  161.7 3.9 %copy-start.6 = (f32[56]{0:T(128)S(1)}, f32[56]{0:T(128)}, u32[]{:S(2)}) copy-start(f32[56]{0:T(128)} %param.9) | copy-start | bytes 676
  161.7 9.0 %copy-start.2 = (s32[56]{0:T(128)S(1)}, s32[56]{0:T(128)}, u32[]{:S(2)}) copy-start(s32[56]{0:T(128)} %param.8) | copy-start | bytes 676
  161.7 7.0 %collective-permute-start.21 = (bf16[56,1536]{1,0:T(8,128)(2,1)S(1)}, bf16[56,1536]{1,0:T(8,128)(2,1)S(1)}, u32[]{:S(2)}, u32[]{:S(2)}) collective-permute-start(bf16[56,1536]{1,0:T(8,128)(2,1)S(1)} %get-tuple-element.25), channel_id=1, source_target_pairs={{0,3},{1,2},{2,1},{3,0},{4,7},{5,6},{6,5},{7,4},{8,11},{9,10},{10,... | collective-permute-start | bytes 516104 | tf_op jit(solution)/shard_map/ppermute | solution.py:31
  165.2 5.5 %collective-permute-start.16 = (bf16[56,1536]{1,0:T(8,128)(2,1)S(1)}, bf16[56,1536]{1,0:T(8,128)(2,1)S(1)}, u32[]{:S(2)}, u32[]{:S(2)}) collective-permute-start(bf16[56,1536]{1,0:T(8,128)(2,1)S(1)} %get-tuple-element.27), channel_id=1, source_target_pairs={{0,1},{1,0},{2,3},{3,2},{4,5},{5,4},{6,7},{7,6},{8,9},{9,8},{10,11... | collective-permute-start | bytes 516104 | tf_op jit(solution)/shard_map/ppermute | solution.py:31

commit v3 on v2

--- a/solution.py
+++ b/solution.py
@@ -36,44 +36,45 @@
 
 
 def shard_order():
-    table = []
-    for g in range(8):
-        z, c = divmod(g, 2)
-        p, q = (P_OFF, Q_OFF) if c == 0 else (Q_OFF, P_OFF)
-        own = [2 * (z ^ o) + c for o in (0, p, q, 2)]
-        other = [2 * (z ^ o) + 1 - c for o in (0, q, p, 2)]
-        table.append(own[:2] + other[:2] + own[2:] + other[2:])
-    return table
+    g = lax.axis_index("grp")
+    z, c = g // 2, g % 2
+    p = jnp.where(c == 0, P_OFF, Q_OFF)
+    q = 4 - p
+    own = [2 * (z ^ o) + c for o in (0, p, q, 2)]
+    other = [2 * (z ^ o) + 1 - c for o in (0, q, p, 2)]
+    return own[:2] + other[:2] + own[2:] + other[2:]
 
 
-def pack(order, routed_slots, tokens):
+def pack(routed_slots, tokens):
     cap, width = routed_slots.shape[0], tokens.shape[1] // 8
 
-    def kernel(order_ref, slots_ref, tokens_ref, a_ref, b_ref):
+    def kernel(slots_ref, tokens_ref, a_ref, b_ref):
         ids = lax.broadcasted_iota(jnp.int32, (tokens.shape[0], cap), 0)
         pick = (ids == slots_ref[...]).astype(F32).T.astype(BF16)
+        order = shard_order()
         for j in range(8):
-            start = pl.multiple_of(order_ref[j] * width, 128)
+            start = pl.multiple_of(order[j] * width, 128)
             part = jnp.dot(pick, tokens_ref[:, pl.ds(start, width)], preferred_element_type=F32).astype(BF16)
             target = a_ref if j < 4 else b_ref
             target[:, (j % 4) * width : (j % 4 + 1) * width] = part
 
     return pl.pallas_call(
         kernel,
-        in_specs=[pl.BlockSpec(memory_space=pltpu.SMEM), pl.BlockSpec(memory_space=pltpu.VMEM), pl.BlockSpec(memory_space=pltpu.VMEM)],
+        in_specs=[pl.BlockSpec(memory_space=pltpu.VMEM), pl.BlockSpec(memory_space=pltpu.VMEM)],
         out_specs=[pl.BlockSpec(memory_space=pltpu.VMEM)] * 2,
         out_shape=[jax.ShapeDtypeStruct((cap, 4 * width), BF16)] * 2,
         compiler_params=pltpu.CompilerParams(vmem_limit_bytes=16 * 2**20),
         name="pack",
-    )(order, routed_slots.reshape(1, cap), tokens)
+    )(routed_slots.reshape(1, cap), tokens)
 
 
-def place(order, routed_slots, combine, pieces, tokens_here):
+def place(routed_slots, combine, pieces, tokens_here):
     cap = routed_slots.shape[0]
     width = pieces[0][0].shape[1] // 2
 
-    def kernel(order_ref, slots_ref, combine_ref, *refs):
+    def kernel(slots_ref, combine_ref, *refs):
         out_ref = refs[-1]
+        order = shard_order()
         ids = lax.broadcasted_iota(jnp.int32, (tokens_here, cap), 0)
         put = (ids == slots_ref[...]).astype(BF16)
         for k in range(4):
@@ -81,18 +82,18 @@
             value = (combine_ref[...] * total).astype(BF16)
             rows = jnp.dot(put, value, preferred_element_type=F32).astype(BF16)
             for i in range(2):
-                start = pl.multiple_of(order_ref[2 * k + i] * width, 128)
+                start = pl.multiple_of(order[2 * k + i] * width, 128)
                 out_ref[:, pl.ds(start, width)] = rows[:, i * width : (i + 1) * width]
 
     flat = [v for pair in pieces for v in pair]
     return pl.pallas_call(
         kernel,
-        in_specs=[pl.BlockSpec(memory_space=pltpu.SMEM)] + [pl.BlockSpec(memory_space=pltpu.VMEM)] * (2 + len(flat)),
+        in_specs=[pl.BlockSpec(memory_space=pltpu.VMEM)] * (2 + len(flat)),
         out_specs=pl.BlockSpec(memory_space=pltpu.VMEM),
         out_shape=jax.ShapeDtypeStruct((tokens_here, 8 * width), BF16),
         compiler_params=pltpu.CompilerParams(vmem_limit_bytes=16 * 2**20),
         name="place",
-    )(order, routed_slots.reshape(1, cap), combine.reshape(cap, 1), *flat)
+    )(routed_slots.reshape(1, cap), combine.reshape(cap, 1), *flat)
 
 
 def dot(a, b):
@@ -113,12 +114,11 @@
 
 
 def on_device(tokens, routed_slots, combine_weight, gate_weight, up_weight, down_weight):
-    order = jnp.asarray(shard_order(), jnp.int32)[lax.axis_index("grp")]
     cap, ff = routed_slots.shape[0], gate_weight.shape[1]
     group = 4 * cap
     p, q = P_OFF, Q_OFF
 
-    own_a, own_b = pack(order, routed_slots, tokens)
+    own_a, own_b = pack(routed_slots, tokens)
     a_1 = stack(own_a, exchange(own_a, "in", p))
     b_1 = stack(own_b, exchange(own_b, "in", q))
     w_0 = jnp.concatenate([gate_weight, up_weight], axis=1)
@@ -162,7 +162,7 @@
             got = exchange(stack(one, block(3)).astype(BF16), "in", off).astype(F32)
             last = exchange((two + got[cap:]).astype(BF16), "in", 4 - off)
             pieces.append((block(0) + got[:cap], last))
-    return place(order, routed_slots, combine_weight, pieces, tokens.shape[0])
+    return place(routed_slots, combine_weight, pieces, tokens.shape[0])
 
 
 def solution(mesh):

time: 173 us -> 172 us (level)
  no operation moved by 1% of the time
where the time goes in v3:
time: 172 us
  waiting for transfers between devices  95.4 us (55%)
  starting transfers between devices  47 us (27%)
  matrix products  19.9 us (12%)
  local copies, waits for them, and re-layouts  3.86 us (2%)
  other arithmetic  2.89 us (2%)
  Pallas kernels  2.2 us (1%)
    ppermute x28, waiting for transfers between devices, exchange(): return lax.ppermute(value, BOTH, PAIRS[kind, off])  95.4 us
    ppermute x28, starting transfers between devices, exchange(): return lax.ppermute(value, BOTH, PAIRS[kind, off])  46.4 us
    dot_general x16, matrix products, dot(): return jnp.dot(a, b, preferred_element_type=F32)  19.9 us
  transfers between devices with their start and end apart: 32, of which 15 were waited for; matrix products, arithmetic and copies ran while one was open for 14% of the time, Pallas kernels for 0%

profile of v3, /device:TPU:0, one launch (start us, length us, event | category | flops | bytes accessed | tf_op | source)
XLA Modules:
  0.0 171.9 jit_solution(11254099530810535803)
XLA Ops:
  0.0 1.4 copy-done
  1.4 0.7 copy-done.1
  2.1 0.4 pack.1
  2.5 1.7 collective-permute-start
  4.4 2.0 %collective-permute-start.8 = (bf16[768,1024]{1,0:T(8,128)(2,1)S(1)}, bf16[768,1024]{1,0:T(8,128)(2,1)S(1)}, u32[]{:S(2)}, u32[]{:S(2)}) collective-permute-start(bf16[768,1024]{1,0:T(8,128)(2,1)S(1)} %constant_dynamic-update-slice_fusion.9), channel_id=1, source_target_pairs={{0,32},{1,33},{2,34},{3,35},{4,36},{5,37},{6,38},{7,39},{8,40},{9,... | collective-permute-start | bytes 4718600 | tf_op jit(solution)/shard_map/ppermute | solution.py:31
  6.4 2.1 %collective-permute-start.4 = (bf16[56,3072]{1,0:T(8,128)(2,1)S(1)}, bf16[56,3072]{1,0:T(8,128)(2,1)S(1)}, u32[]{:S(2)}, u32[]{:S(2)}) collective-permute-start(bf16[56,3072]{1,0:T(8,128)(2,1)S(1)} %get-tuple-element.12), channel_id=1, source_target_pairs={{0,3},{1,2},{2,1},{3,0},{4,7},{5,6},{6,5},{7,4},{8,11},{9,10},{10,... | collective-permute-start | bytes 1032200 | tf_op jit(solution)/shard_map/ppermute | solution.py:31
  8.7 1.2 collective-permute-done
  9.9 2.9 %collective-permute-start.1 = (bf16[112,3072]{1,0:T(8,128)(2,1)S(1)}, bf16[112,3072]{1,0:T(8,128)(2,1)S(1)}, u32[]{:S(2)}, u32[]{:S(2)}) collective-permute-start(bf16[112,3072]{1,0:T(8,128)(2,1)S(1)} %pad_maximum_fusion.3), channel_id=1, source_target_pairs={{0,3},{1,2},{2,1},{3,0},{4,7},{5,6},{6,5},{7,4},{8,11},{9,10},{10,... | collective-permute-start | bytes 2064392 | tf_op jit(solution)/shard_map/ppermute | solution.py:31
  12.8 2.1 %collective-permute-done.4 = bf16[56,3072]{1,0:T(8,128)(2,1)S(1)} collective-permute-done((bf16[56,3072]{1,0:T(8,128)(2,1)S(1)}, bf16[56,3072]{1,0:T(8,128)(2,1)S(1)}, u32[]{:S(2)}, u32[]{:S(2)}) %collective-permute-start.4) | collective-permute-done | bytes 344096 | tf_op jit(solution)/shard_map/ppermute | solution.py:31
  15.0 7.2 %collective-permute-done.1 = bf16[112,3072]{1,0:T(8,128)(2,1)S(1)} collective-permute-done((bf16[112,3072]{1,0:T(8,128)(2,1)S(1)}, bf16[112,3072]{1,0:T(8,128)(2,1)S(1)}, u32[]{:S(2)}, u32[]{:S(2)}) %collective-permute-start.1) | collective-permute-done | bytes 688160 | tf_op jit(solution)/shard_map/ppermute | solution.py:31
  22.3 1.7 collective-permute-start.2
  24.0 0.9 collective-permute-done.8
  24.9 0.3 pad_maximum_fusion
  25.2 4.1 %collective-permute-start.10 = (bf16[1536,1024]{1,0:T(8,128)(2,1)S(1)}, bf16[1536,1024]{1,0:T(8,128)(2,1)S(1)}, u32[]{:S(2)}, u32[]{:S(2)}) collective-permute-start(bf16[1536,1024]{1,0:T(8,128)(2,1)S(1)} %pad_maximum_fusion), channel_id=1, source_target_pairs={{0,96},{1,97},{2,98},{3,99},{4,100},{5,101},{6,102},{7,103},{8,104... | collective-permute-start | bytes 9437192 | tf_op jit(solution)/shard_map/ppermute | solution.py:31
  29.6 3.1 %collective-permute-start.6 = (bf16[224,3072]{1,0:T(8,128)(2,1)S(1)}, bf16[224,3072]{1,0:T(8,128)(2,1)S(1)}, u32[]{:S(2)}, u32[]{:S(2)}) collective-permute-start(bf16[224,3072]{1,0:T(8,128)(2,1)S(1)} %pad_maximum_fusion.2), channel_id=1, source_target_pairs={{0,12},{1,13},{2,14},{3,15},{4,8},{5,9},{6,10},{7,11},{8,4},{9,5},... | collective-permute-start | bytes 4128776 | tf_op jit(solution)/shard_map/ppermute | solution.py:31
  32.9 16.3 %collective-permute-done.6 = bf16[224,3072]{1,0:T(8,128)(2,1)S(1)} collective-permute-done((bf16[224,3072]{1,0:T(8,128)(2,1)S(1)}, bf16[224,3072]{1,0:T(8,128)(2,1)S(1)}, u32[]{:S(2)}, u32[]{:S(2)}) %collective-permute-start.6) | collective-permute-done | bytes 1376288 | tf_op jit(solution)/shard_map/ppermute | solution.py:31
  49.2 0.4 collective-permute-start.7
  49.8 2.8 %collective-permute-start.3 = (bf16[448,3072]{1,0:T(8,128)(2,1)S(1)}, bf16[448,3072]{1,0:T(8,128)(2,1)S(1)}, u32[]{:S(2)}, u32[]{:S(2)}) collective-permute-start(bf16[448,3072]{1,0:T(8,128)(2,1)S(1)} %constant_dynamic-update-slice_fusion), channel_id=1, source_target_pairs={{0,12},{1,13},{2,14},{3,15},{4,8},{5,9},{6,10},{7,11},{8,4},{9,5},... | collective-permute-start | bytes 8257544 | tf_op jit(solution)/shard_map/ppermute | solution.py:31
  52.7 1.2 collective-permute-start.22
  53.8 14.2 %collective-permute-done.10 = bf16[1536,1024]{1,0:T(8,128)(2,1)S(1)} collective-permute-done((bf16[1536,1024]{1,0:T(8,128)(2,1)S(1)}, bf16[1536,1024]{1,0:T(8,128)(2,1)S(1)}, u32[]{:S(2)}, u32[]{:S(2)}) %collective-permute-start.10) | collective-permute-done | bytes 3145760 | tf_op jit(solution)/shard_map/ppermute | solution.py:31
  68.0 1.6 fusion.1
  69.6 15.2 %collective-permute-done.22 = bf16[512,1536]{1,0:T(8,128)(2,1)S(1)} collective-permute-done((bf16[512,1536]{1,0:T(8,128)(2,1)S(1)}, bf16[512,1536]{1,0:T(8,128)(2,1)S(1)}, u32[]{:S(2)}, u32[]{:S(2)}) %collective-permute-start.22) | collective-permute-done | bytes 1572896 | tf_op jit(solution)/shard_map/ppermute | solution.py:31
  84.9 0.5 collective-permute-start.27
  85.4 1.6 fusion.3
  87.0 1.6 convolution_add_fusion.6
  88.6 1.6 fusion.6
  90.2 1.6 fusion.10
  91.8 1.6 convolution_add_fusion.4
  93.5 1.6 convolution_add_fusion.5
  95.1 0.4 fusion.24
  95.5 1.6 maximum_add_fusion.1
  97.5 0.3 maximum_add_fusion
  98.1 0.9 convolution_convert_fusion
  99.0 1.1 collective-permute-start.28
  100.1 0.9 convolution_convert_fusion.1
  101.0 2.5 %collective-permute-start.23 = (bf16[448,1536]{1,0:T(8,128)(2,1)S(1)}, bf16[448,1536]{1,0:T(8,128)(2,1)S(1)}, u32[]{:S(2)}, u32[]{:S(2)}) collective-permute-start(bf16[448,1536]{1,0:T(8,128)(2,1)S(1)} %convolution_convert_fusion.1), channel_id=1, source_target_pairs={{0,12},{1,13},{2,14},{3,15},{4,8},{5,9},{6,10},{7,11},{8,4},{9,5},... | collective-permute-start | bytes 4128776 | tf_op jit(solution)/shard_map/ppermute | solution.py:31
  103.5 0.9 convolution_convert_fusion.2
  104.4 0.7 collective-permute-start.18
  105.1 0.9 convolution_convert_fusion.3
  106.0 0.9 collective-permute-start.13
  106.9 10.5 %collective-permute-done.28 = bf16[448,1536]{1,0:T(8,128)(2,1)S(1)} collective-permute-done((bf16[448,1536]{1,0:T(8,128)(2,1)S(1)}, bf16[448,1536]{1,0:T(8,128)(2,1)S(1)}, u32[]{:S(2)}, u32[]{:S(2)}) %collective-permute-start.28) | collective-permute-done | bytes 1376288 | tf_op jit(solution)/shard_map/ppermute | solution.py:31
  117.4 0.9 convolution_add_fusion
  118.4 2.5 %collective-permute-start.29 = (bf16[224,1536]{1,0:T(8,128)(2,1)S(1)}, bf16[224,1536]{1,0:T(8,128)(2,1)S(1)}, u32[]{:S(2)}, u32[]{:S(2)}) collective-permute-start(bf16[224,1536]{1,0:T(8,128)(2,1)S(1)} %slice.320), channel_id=1, source_target_pairs={{0,12},{1,13},{2,14},{3,15},{4,8},{5,9},{6,10},{7,11},{8,4},{9,5},... | collective-permute-start | bytes 2064392 | tf_op jit(solution)/shard_map/ppermute | solution.py:31
  120.9 0.9 convolution_add_fusion.1
  121.9 0.5 collective-permute-start.24
  122.4 9.8 %collective-permute-done.18 = bf16[448,1536]{1,0:T(8,128)(2,1)S(1)} collective-permute-done((bf16[448,1536]{1,0:T(8,128)(2,1)S(1)}, bf16[448,1536]{1,0:T(8,128)(2,1)S(1)}, u32[]{:S(2)}, u32[]{:S(2)}) %collective-permute-start.18) | collective-permute-done | bytes 1376288 | tf_op jit(solution)/shard_map/ppermute | solution.py:31
  132.2 0.9 convolution_add_fusion.2
  133.1 2.5 %collective-permute-start.19 = (bf16[224,1536]{1,0:T(8,128)(2,1)S(1)}, bf16[224,1536]{1,0:T(8,128)(2,1)S(1)}, u32[]{:S(2)}, u32[]{:S(2)}) collective-permute-start(bf16[224,1536]{1,0:T(8,128)(2,1)S(1)} %slice.322), channel_id=1, source_target_pairs={{0,12},{1,13},{2,14},{3,15},{4,8},{5,9},{6,10},{7,11},{8,4},{9,5},... | collective-permute-start | bytes 2064392 | tf_op jit(solution)/shard_map/ppermute | solution.py:31
  135.7 0.9 convolution_add_fusion.3
  136.6 0.5 collective-permute-start.14
  137.1 5.6 %collective-permute-done.29 = bf16[224,1536]{1,0:T(8,128)(2,1)S(1)} collective-permute-done((bf16[224,1536]{1,0:T(8,128)(2,1)S(1)}, bf16[224,1536]{1,0:T(8,128)(2,1)S(1)}, u32[]{:S(2)}, u32[]{:S(2)}) %collective-permute-start.29) | collective-permute-done | bytes 688160 | tf_op jit(solution)/shard_map/ppermute | solution.py:31
  143.0 1.6 collective-permute-start.30
  144.8 2.2 %collective-permute-start.25 = (bf16[112,1536]{1,0:T(8,128)(2,1)S(1)}, bf16[112,1536]{1,0:T(8,128)(2,1)S(1)}, u32[]{:S(2)}, u32[]{:S(2)}) collective-permute-start(bf16[112,1536]{1,0:T(8,128)(2,1)S(1)} %concatenate.77), channel_id=1, source_target_pairs={{0,3},{1,2},{2,1},{3,0},{4,7},{5,6},{6,5},{7,4},{8,11},{9,10},{10,... | collective-permute-start | bytes 1032200 | tf_op jit(solution)/shard_map/ppermute | solution.py:31
  147.0 6.2 %collective-permute-done.19 = bf16[224,1536]{1,0:T(8,128)(2,1)S(1)} collective-permute-done((bf16[224,1536]{1,0:T(8,128)(2,1)S(1)}, bf16[224,1536]{1,0:T(8,128)(2,1)S(1)}, u32[]{:S(2)}, u32[]{:S(2)}) %collective-permute-start.19) | collective-permute-done | bytes 688160 | tf_op jit(solution)/shard_map/ppermute | solution.py:31
  153.4 2.2 %collective-permute-start.20 = (bf16[112,1536]{1,0:T(8,128)(2,1)S(1)}, bf16[112,1536]{1,0:T(8,128)(2,1)S(1)}, u32[]{:S(2)}, u32[]{:S(2)}) collective-permute-start(bf16[112,1536]{1,0:T(8,128)(2,1)S(1)} %pad_maximum_fusion.7), channel_id=1, source_target_pairs={{0,1},{1,0},{2,3},{3,2},{4,5},{5,4},{6,7},{7,6},{8,9},{9,8},{10,11... | collective-permute-start | bytes 1032200 | tf_op jit(solution)/shard_map/ppermute | solution.py:31
  155.8 2.2 %collective-permute-start.15 = (bf16[112,1536]{1,0:T(8,128)(2,1)S(1)}, bf16[112,1536]{1,0:T(8,128)(2,1)S(1)}, u32[]{:S(2)}, u32[]{:S(2)}) collective-permute-start(bf16[112,1536]{1,0:T(8,128)(2,1)S(1)} %concatenate.78), channel_id=1, source_target_pairs={{0,3},{1,2},{2,1},{3,0},{4,7},{5,6},{6,5},{7,4},{8,11},{9,10},{10,... | collective-permute-start | bytes 1032200 | tf_op jit(solution)/shard_map/ppermute | solution.py:31
  158.2 1.2 collective-permute-start.31
  159.7 1.2 collective-permute-done.20
  161.1 3.4 %collective-permute-start.21 = (bf16[56,1536]{1,0:T(8,128)(2,1)S(1)}, bf16[56,1536]{1,0:T(8,128)(2,1)S(1)}, u32[]{:S(2)}, u32[]{:S(2)}) collective-permute-start(bf16[56,1536]{1,0:T(8,128)(2,1)S(1)} %get-tuple-element.25), channel_id=1, source_target_pairs={{0,3},{1,2},{2,1},{3,0},{4,7},{5,6},{6,5},{7,4},{8,11},{9,10},{10,... | collective-permute-start | bytes 516104 | tf_op jit(solution)/shard_map/ppermute | solution.py:31
  164.6 0.3 collective-permute-start.16
  165.0 1.2 collective-permute-done.31.refs_7_
  166.2 1.8 %collective-permute-done.21.refs_3_ = bf16[56,1536]{1,0:T(8,128)(2,1)S(1)} collective-permute-done((bf16[56,1536]{1,0:T(8,128)(2,1)S(1)}, bf16[56,1536]{1,0:T(8,128)(2,1)S(1)}, u32[]{:S(2)}, u32[]{:S(2)}) %collective-permute-start.21) | collective-permute-done | bytes 172064 | tf_op jit(solution)/shard_map/ppermute | solution.py:31
  168.1 2.0 %collective-permute-done.16.refs_1_ = bf16[56,1536]{1,0:T(8,128)(2,1)S(1)} collective-permute-done((bf16[56,1536]{1,0:T(8,128)(2,1)S(1)}, bf16[56,1536]{1,0:T(8,128)(2,1)S(1)}, u32[]{:S(2)}, u32[]{:S(2)}) %collective-permute-start.16) | collective-permute-done | bytes 172064 | tf_op jit(solution)/shard_map/ppermute | solution.py:31
  170.1 1.8 %place.1 = bf16[128,6144]{1,0:T(8,128)(2,1)} custom-call(s32[1,56]{1,0:T(1,128)S(1)} %bitcast.21, f32[56,1]{1,0:T(8,128)S(1)} %copy.7.combine_ref, f32[56,1536]{1,0:T(8,128)S(1)} %get-tuple-element.28.refs_0_, bf16[56,1536]{1,0:T(8,128)(2,1)S(1)} %collective-permute-done.16.refs_1_, f32[56,1536]{1,0:T(8,128)S(1)} %get-tuple-element.26.refs_2_, ...), custom_call_target="tpu_custom_call" | custom-call | tf_op jit(solution)/shard_map/place/pallas_call | solution.py:89
  (79 shorter events, 4.0 us)
Async XLA Ops:
  0.0 1.4 copy-start
  1.4 0.7 copy-start.1
  2.1 2.1 %copy-start.3 = (bf16[768,512]{1,0:T(8,128)(2,1)S(1)}, bf16[768,512]{1,0:T(8,128)(2,1)}, u32[]{:S(2)}) copy-start(bf16[768,512]{1,0:T(8,128)(2,1)} %param.9) | copy-start | bytes 2359300
  2.1 2.2 %copy-start.4 = (bf16[768,512]{1,0:T(8,128)(2,1)S(1)}, bf16[768,512]{1,0:T(8,128)(2,1)}, u32[]{:S(2)}) copy-start(bf16[768,512]{1,0:T(8,128)(2,1)} %param.10) | copy-start | bytes 2359300
  2.5 6.0 %copy-start.5 = (bf16[512,768]{1,0:T(8,128)(2,1)S(1)}, bf16[512,768]{1,0:T(8,128)(2,1)}, u32[]{:S(2)}) copy-start(bf16[512,768]{1,0:T(8,128)(2,1)} %param.11) | copy-start | bytes 2359300
  2.5 7.3 %collective-permute-start = (bf16[56,3072]{1,0:T(8,128)(2,1)S(1)}, bf16[56,3072]{1,0:T(8,128)(2,1)S(1)}, u32[]{:S(2)}, u32[]{:S(2)}) collective-permute-start(bf16[56,3072]{1,0:T(8,128)(2,1)S(1)} %get-tuple-element.11), channel_id=1, source_target_pairs={{0,1},{1,0},{2,3},{3,2},{4,5},{5,4},{6,7},{7,6},{8,9},{9,8},{10,11... | collective-permute-start | bytes 1032200 | tf_op jit(solution)/shard_map/ppermute | solution.py:31
  4.4 20.5 %collective-permute-start.8 = (bf16[768,1024]{1,0:T(8,128)(2,1)S(1)}, bf16[768,1024]{1,0:T(8,128)(2,1)S(1)}, u32[]{:S(2)}, u32[]{:S(2)}) collective-permute-start(bf16[768,1024]{1,0:T(8,128)(2,1)S(1)} %constant_dynamic-update-slice_fusion.9), channel_id=1, source_target_pairs={{0,32},{1,33},{2,34},{3,35},{4,36},{5,37},{6,38},{7,39},{8,40},{9,... | collective-permute-start | bytes 4718600 | tf_op jit(solution)/shard_map/ppermute | solution.py:31
  6.4 8.5 %collective-permute-start.4 = (bf16[56,3072]{1,0:T(8,128)(2,1)S(1)}, bf16[56,3072]{1,0:T(8,128)(2,1)S(1)}, u32[]{:S(2)}, u32[]{:S(2)}) collective-permute-start(bf16[56,3072]{1,0:T(8,128)(2,1)S(1)} %get-tuple-element.12), channel_id=1, source_target_pairs={{0,3},{1,2},{2,1},{3,0},{4,7},{5,6},{6,5},{7,4},{8,11},{9,10},{10,... | collective-permute-start | bytes 1032200 | tf_op jit(solution)/shard_map/ppermute | solution.py:31
  8.5 44.1 %collective-permute-start.12 = (bf16[512,768]{1,0:T(8,128)(2,1)S(1)}, bf16[512,768]{1,0:T(8,128)(2,1)S(1)}, u32[]{:S(2)}, u32[]{:S(2)}) collective-permute-start(bf16[512,768]{1,0:T(8,128)(2,1)S(1)} %copy-done.5), channel_id=1, source_target_pairs={{0,32},{1,33},{2,34},{3,35},{4,36},{5,37},{6,38},{7,39},{8,40},{9,... | collective-permute-start | bytes 2359304 | tf_op jit(solution)/shard_map/ppermute | solution.py:31
  9.9 12.3 %collective-permute-start.1 = (bf16[112,3072]{1,0:T(8,128)(2,1)S(1)}, bf16[112,3072]{1,0:T(8,128)(2,1)S(1)}, u32[]{:S(2)}, u32[]{:S(2)}) collective-permute-start(bf16[112,3072]{1,0:T(8,128)(2,1)S(1)} %pad_maximum_fusion.3), channel_id=1, source_target_pairs={{0,3},{1,2},{2,1},{3,0},{4,7},{5,6},{6,5},{7,4},{8,11},{9,10},{10,... | collective-permute-start | bytes 2064392 | tf_op jit(solution)/shard_map/ppermute | solution.py:31
  14.9 14.4 %collective-permute-start.5 = (bf16[112,3072]{1,0:T(8,128)(2,1)S(1)}, bf16[112,3072]{1,0:T(8,128)(2,1)S(1)}, u32[]{:S(2)}, u32[]{:S(2)}) collective-permute-start(bf16[112,3072]{1,0:T(8,128)(2,1)S(1)} %pad_maximum_fusion.4), channel_id=1, source_target_pairs={{0,1},{1,0},{2,3},{3,2},{4,5},{5,4},{6,7},{7,6},{8,9},{9,8},{10,11... | collective-permute-start | bytes 2064392 | tf_op jit(solution)/shard_map/ppermute | solution.py:31
  22.3 27.4 %collective-permute-start.2 = (bf16[224,3072]{1,0:T(8,128)(2,1)S(1)}, bf16[224,3072]{1,0:T(8,128)(2,1)S(1)}, u32[]{:S(2)}, u32[]{:S(2)}) collective-permute-start(bf16[224,3072]{1,0:T(8,128)(2,1)S(1)} %pad_maximum_fusion.1), channel_id=1, source_target_pairs={{0,4},{1,5},{2,6},{3,7},{4,0},{5,1},{6,2},{7,3},{8,12},{9,13},{10,... | collective-permute-start | bytes 4128776 | tf_op jit(solution)/shard_map/ppermute | solution.py:31
  25.2 42.8 %collective-permute-start.10 = (bf16[1536,1024]{1,0:T(8,128)(2,1)S(1)}, bf16[1536,1024]{1,0:T(8,128)(2,1)S(1)}, u32[]{:S(2)}, u32[]{:S(2)}) collective-permute-start(bf16[1536,1024]{1,0:T(8,128)(2,1)S(1)} %pad_maximum_fusion), channel_id=1, source_target_pairs={{0,96},{1,97},{2,98},{3,99},{4,100},{5,101},{6,102},{7,103},{8,104... | collective-permute-start | bytes 9437192 | tf_op jit(solution)/shard_map/ppermute | solution.py:31
  29.6 19.6 %collective-permute-start.6 = (bf16[224,3072]{1,0:T(8,128)(2,1)S(1)}, bf16[224,3072]{1,0:T(8,128)(2,1)S(1)}, u32[]{:S(2)}, u32[]{:S(2)}) collective-permute-start(bf16[224,3072]{1,0:T(8,128)(2,1)S(1)} %pad_maximum_fusion.2), channel_id=1, source_target_pairs={{0,12},{1,13},{2,14},{3,15},{4,8},{5,9},{6,10},{7,11},{8,4},{9,5},... | collective-permute-start | bytes 4128776 | tf_op jit(solution)/shard_map/ppermute | solution.py:31
  32.7 52.1 %collective-permute-start.9 = (bf16[1536,1024]{1,0:T(8,128)(2,1)S(1)}, bf16[1536,1024]{1,0:T(8,128)(2,1)S(1)}, u32[]{:S(2)}, u32[]{:S(2)}) collective-permute-start(bf16[1536,1024]{1,0:T(8,128)(2,1)S(1)} %pad_maximum_fusion), channel_id=1, source_target_pairs={{0,16},{1,17},{2,18},{3,19},{4,20},{5,21},{6,22},{7,23},{8,24},{9,... | collective-permute-start | bytes 9437192 | tf_op jit(solution)/shard_map/ppermute | solution.py:35
  49.2 39.3 %collective-permute-start.7 = (bf16[448,3072]{1,0:T(8,128)(2,1)S(1)}, bf16[448,3072]{1,0:T(8,128)(2,1)S(1)}, u32[]{:S(2)}, u32[]{:S(2)}) collective-permute-start(bf16[448,3072]{1,0:T(8,128)(2,1)S(1)} %constant_dynamic-update-slice_fusion.4), channel_id=1, source_target_pairs={{0,4},{1,5},{2,6},{3,7},{4,0},{5,1},{6,2},{7,3},{8,12},{9,13},{10,... | collective-permute-start | bytes 8257544 | tf_op jit(solution)/shard_map/ppermute | solution.py:31
  49.8 38.8 %collective-permute-start.3 = (bf16[448,3072]{1,0:T(8,128)(2,1)S(1)}, bf16[448,3072]{1,0:T(8,128)(2,1)S(1)}, u32[]{:S(2)}, u32[]{:S(2)}) collective-permute-start(bf16[448,3072]{1,0:T(8,128)(2,1)S(1)} %constant_dynamic-update-slice_fusion), channel_id=1, source_target_pairs={{0,12},{1,13},{2,14},{3,15},{4,8},{5,9},{6,10},{7,11},{8,4},{9,5},... | collective-permute-start | bytes 8257544 | tf_op jit(solution)/shard_map/ppermute | solution.py:31
  52.7 32.2 %collective-permute-start.22 = (bf16[512,1536]{1,0:T(8,128)(2,1)S(1)}, bf16[512,1536]{1,0:T(8,128)(2,1)S(1)}, u32[]{:S(2)}, u32[]{:S(2)}) collective-permute-start(bf16[512,1536]{1,0:T(8,128)(2,1)S(1)} %constant_dynamic-update-slice_fusion.11), channel_id=1, source_target_pairs={{0,96},{1,97},{2,98},{3,99},{4,100},{5,101},{6,102},{7,103},{8,104... | collective-permute-start | bytes 4718600 | tf_op jit(solution)/shard_map/ppermute | solution.py:31
  68.0 23.8 %collective-permute-start.11 = (bf16[1536,1024]{1,0:T(8,128)(2,1)S(1)}, bf16[1536,1024]{1,0:T(8,128)(2,1)S(1)}, u32[]{:S(2)}, u32[]{:S(2)}) collective-permute-start(bf16[1536,1024]{1,0:T(8,128)(2,1)S(1)} %collective-permute-done.10), channel_id=1, source_target_pairs={{0,16},{1,17},{2,18},{3,19},{4,20},{5,21},{6,22},{7,23},{8,24},{9,... | collective-permute-start | bytes 9437192 | tf_op jit(solution)/shard_map/ppermute | solution.py:35
  84.8 18.7 %collective-permute-start.17 = (bf16[512,1536]{1,0:T(8,128)(2,1)S(1)}, bf16[512,1536]{1,0:T(8,128)(2,1)S(1)}, u32[]{:S(2)}, u32[]{:S(2)}) collective-permute-start(bf16[512,1536]{1,0:T(8,128)(2,1)S(1)} %constant_dynamic-update-slice_fusion.11), channel_id=1, source_target_pairs={{0,16},{1,17},{2,18},{3,19},{4,20},{5,21},{6,22},{7,23},{8,24},{9,... | collective-permute-start | bytes 4718600 | tf_op jit(solution)/shard_map/ppermute | solution.py:35
  84.9 13.3 %collective-permute-start.27 = (bf16[512,1536]{1,0:T(8,128)(2,1)S(1)}, bf16[512,1536]{1,0:T(8,128)(2,1)S(1)}, u32[]{:S(2)}, u32[]{:S(2)}) collective-permute-start(bf16[512,1536]{1,0:T(8,128)(2,1)S(1)} %collective-permute-done.22), channel_id=1, source_target_pairs={{0,16},{1,17},{2,18},{3,19},{4,20},{5,21},{6,22},{7,23},{8,24},{9,... | collective-permute-start | bytes 4718600 | tf_op jit(solution)/shard_map/ppermute | solution.py:35
  99.0 18.4 %collective-permute-start.28 = (bf16[448,1536]{1,0:T(8,128)(2,1)S(1)}, bf16[448,1536]{1,0:T(8,128)(2,1)S(1)}, u32[]{:S(2)}, u32[]{:S(2)}) collective-permute-start(bf16[448,1536]{1,0:T(8,128)(2,1)S(1)} %convolution_convert_fusion), channel_id=1, source_target_pairs={{0,4},{1,5},{2,6},{3,7},{4,0},{5,1},{6,2},{7,3},{8,12},{9,13},{10,... | collective-permute-start | bytes 4128776 | tf_op jit(solution)/shard_map/ppermute | solution.py:31
  101.0 19.9 %collective-permute-start.23 = (bf16[448,1536]{1,0:T(8,128)(2,1)S(1)}, bf16[448,1536]{1,0:T(8,128)(2,1)S(1)}, u32[]{:S(2)}, u32[]{:S(2)}) collective-permute-start(bf16[448,1536]{1,0:T(8,128)(2,1)S(1)} %convolution_convert_fusion.1), channel_id=1, source_target_pairs={{0,12},{1,13},{2,14},{3,15},{4,8},{5,9},{6,10},{7,11},{8,4},{9,5},... | collective-permute-start | bytes 4128776 | tf_op jit(solution)/shard_map/ppermute | solution.py:31
  104.4 27.7 %collective-permute-start.18 = (bf16[448,1536]{1,0:T(8,128)(2,1)S(1)}, bf16[448,1536]{1,0:T(8,128)(2,1)S(1)}, u32[]{:S(2)}, u32[]{:S(2)}) collective-permute-start(bf16[448,1536]{1,0:T(8,128)(2,1)S(1)} %convolution_convert_fusion.2), channel_id=1, source_target_pairs={{0,4},{1,5},{2,6},{3,7},{4,0},{5,1},{6,2},{7,3},{8,12},{9,13},{10,... | collective-permute-start | bytes 4128776 | tf_op jit(solution)/shard_map/ppermute | solution.py:31
  106.0 29.6 %collective-permute-start.13 = (bf16[448,1536]{1,0:T(8,128)(2,1)S(1)}, bf16[448,1536]{1,0:T(8,128)(2,1)S(1)}, u32[]{:S(2)}, u32[]{:S(2)}) collective-permute-start(bf16[448,1536]{1,0:T(8,128)(2,1)S(1)} %convolution_convert_fusion.3), channel_id=1, source_target_pairs={{0,12},{1,13},{2,14},{3,15},{4,8},{5,9},{6,10},{7,11},{8,4},{9,5},... | collective-permute-start | bytes 4128776 | tf_op jit(solution)/shard_map/ppermute | solution.py:31
  118.4 24.3 %collective-permute-start.29 = (bf16[224,1536]{1,0:T(8,128)(2,1)S(1)}, bf16[224,1536]{1,0:T(8,128)(2,1)S(1)}, u32[]{:S(2)}, u32[]{:S(2)}) collective-permute-start(bf16[224,1536]{1,0:T(8,128)(2,1)S(1)} %slice.320), channel_id=1, source_target_pairs={{0,12},{1,13},{2,14},{3,15},{4,8},{5,9},{6,10},{7,11},{8,4},{9,5},... | collective-permute-start | bytes 2064392 | tf_op jit(solution)/shard_map/ppermute | solution.py:31
  121.9 22.7 %collective-permute-start.24 = (bf16[224,1536]{1,0:T(8,128)(2,1)S(1)}, bf16[224,1536]{1,0:T(8,128)(2,1)S(1)}, u32[]{:S(2)}, u32[]{:S(2)}) collective-permute-start(bf16[224,1536]{1,0:T(8,128)(2,1)S(1)} %slice.321), channel_id=1, source_target_pairs={{0,4},{1,5},{2,6},{3,7},{4,0},{5,1},{6,2},{7,3},{8,12},{9,13},{10,... | collective-permute-start | bytes 2064392 | tf_op jit(solution)/shard_map/ppermute | solution.py:31
  133.1 20.0 %collective-permute-start.19 = (bf16[224,1536]{1,0:T(8,128)(2,1)S(1)}, bf16[224,1536]{1,0:T(8,128)(2,1)S(1)}, u32[]{:S(2)}, u32[]{:S(2)}) collective-permute-start(bf16[224,1536]{1,0:T(8,128)(2,1)S(1)} %slice.322), channel_id=1, source_target_pairs={{0,12},{1,13},{2,14},{3,15},{4,8},{5,9},{6,10},{7,11},{8,4},{9,5},... | collective-permute-start | bytes 2064392 | tf_op jit(solution)/shard_map/ppermute | solution.py:31
  136.6 19.0 %collective-permute-start.14 = (bf16[224,1536]{1,0:T(8,128)(2,1)S(1)}, bf16[224,1536]{1,0:T(8,128)(2,1)S(1)}, u32[]{:S(2)}, u32[]{:S(2)}) collective-permute-start(bf16[224,1536]{1,0:T(8,128)(2,1)S(1)} %slice.323), channel_id=1, source_target_pairs={{0,4},{1,5},{2,6},{3,7},{4,0},{5,1},{6,2},{7,3},{8,12},{9,13},{10,... | collective-permute-start | bytes 2064392 | tf_op jit(solution)/shard_map/ppermute | solution.py:31
  143.0 15.0 %collective-permute-start.30 = (bf16[112,1536]{1,0:T(8,128)(2,1)S(1)}, bf16[112,1536]{1,0:T(8,128)(2,1)S(1)}, u32[]{:S(2)}, u32[]{:S(2)}) collective-permute-start(bf16[112,1536]{1,0:T(8,128)(2,1)S(1)} %pad_maximum_fusion.8), channel_id=1, source_target_pairs={{0,1},{1,0},{2,3},{3,2},{4,5},{5,4},{6,7},{7,6},{8,9},{9,8},{10,11... | collective-permute-start | bytes 1032200 | tf_op jit(solution)/shard_map/ppermute | solution.py:31
  144.8 14.6 %collective-permute-start.25 = (bf16[112,1536]{1,0:T(8,128)(2,1)S(1)}, bf16[112,1536]{1,0:T(8,128)(2,1)S(1)}, u32[]{:S(2)}, u32[]{:S(2)}) collective-permute-start(bf16[112,1536]{1,0:T(8,128)(2,1)S(1)} %concatenate.77), channel_id=1, source_target_pairs={{0,3},{1,2},{2,1},{3,0},{4,7},{5,6},{6,5},{7,4},{8,11},{9,10},{10,... | collective-permute-start | bytes 1032200 | tf_op jit(solution)/shard_map/ppermute | solution.py:31
  153.4 7.4 %collective-permute-start.20 = (bf16[112,1536]{1,0:T(8,128)(2,1)S(1)}, bf16[112,1536]{1,0:T(8,128)(2,1)S(1)}, u32[]{:S(2)}, u32[]{:S(2)}) collective-permute-start(bf16[112,1536]{1,0:T(8,128)(2,1)S(1)} %pad_maximum_fusion.7), channel_id=1, source_target_pairs={{0,1},{1,0},{2,3},{3,2},{4,5},{5,4},{6,7},{7,6},{8,9},{9,8},{10,11... | collective-permute-start | bytes 1032200 | tf_op jit(solution)/shard_map/ppermute | solution.py:31
  155.8 8.6 %collective-permute-start.15 = (bf16[112,1536]{1,0:T(8,128)(2,1)S(1)}, bf16[112,1536]{1,0:T(8,128)(2,1)S(1)}, u32[]{:S(2)}, u32[]{:S(2)}) collective-permute-start(bf16[112,1536]{1,0:T(8,128)(2,1)S(1)} %concatenate.78), channel_id=1, source_target_pairs={{0,3},{1,2},{2,1},{3,0},{4,7},{5,6},{6,5},{7,4},{8,11},{9,10},{10,... | collective-permute-start | bytes 1032200 | tf_op jit(solution)/shard_map/ppermute | solution.py:31
  158.2 8.0 %collective-permute-start.31 = (bf16[56,1536]{1,0:T(8,128)(2,1)S(1)}, bf16[56,1536]{1,0:T(8,128)(2,1)S(1)}, u32[]{:S(2)}, u32[]{:S(2)}) collective-permute-start(bf16[56,1536]{1,0:T(8,128)(2,1)S(1)} %get-tuple-element.21), channel_id=1, source_target_pairs={{0,3},{1,2},{2,1},{3,0},{4,7},{5,6},{6,5},{7,4},{8,11},{9,10},{10,... | collective-permute-start | bytes 516104 | tf_op jit(solution)/shard_map/ppermute | solution.py:31
  159.6 6.6 %collective-permute-start.26 = (bf16[56,1536]{1,0:T(8,128)(2,1)S(1)}, bf16[56,1536]{1,0:T(8,128)(2,1)S(1)}, u32[]{:S(2)}, u32[]{:S(2)}) collective-permute-start(bf16[56,1536]{1,0:T(8,128)(2,1)S(1)} %get-tuple-element.23), channel_id=1, source_target_pairs={{0,1},{1,0},{2,3},{3,2},{4,5},{5,4},{6,7},{7,6},{8,9},{9,8},{10,11... | collective-permute-start | bytes 516104 | tf_op jit(solution)/shard_map/ppermute | solution.py:31
  161.0 3.9 %copy-start.6 = (f32[56]{0:T(128)S(1)}, f32[56]{0:T(128)}, u32[]{:S(2)}) copy-start(f32[56]{0:T(128)} %param.8) | copy-start | bytes 676
  161.0 9.0 %copy-start.2 = (s32[56]{0:T(128)S(1)}, s32[56]{0:T(128)}, u32[]{:S(2)}) copy-start(s32[56]{0:T(128)} %param.7) | copy-start | bytes 676
  161.1 7.0 %collective-permute-start.21 = (bf16[56,1536]{1,0:T(8,128)(2,1)S(1)}, bf16[56,1536]{1,0:T(8,128)(2,1)S(1)}, u32[]{:S(2)}, u32[]{:S(2)}) collective-permute-start(bf16[56,1536]{1,0:T(8,128)(2,1)S(1)} %get-tuple-element.25), channel_id=1, source_target_pairs={{0,3},{1,2},{2,1},{3,0},{4,7},{5,6},{6,5},{7,4},{8,11},{9,10},{10,... | collective-permute-start | bytes 516104 | tf_op jit(solution)/shard_map/ppermute | solution.py:31
  164.6 5.5 %collective-permute-start.16 = (bf16[56,1536]{1,0:T(8,128)(2,1)S(1)}, bf16[56,1536]{1,0:T(8,128)(2,1)S(1)}, u32[]{:S(2)}, u32[]{:S(2)}) collective-permute-start(bf16[56,1536]{1,0:T(8,128)(2,1)S(1)} %get-tuple-element.27), channel_id=1, source_target_pairs={{0,1},{1,0},{2,3},{3,2},{4,5},{5,4},{6,7},{7,6},{8,9},{9,8},{10,11... | collective-permute-start | bytes 516104 | tf_op jit(solution)/shard_map/ppermute | solution.py:31

commit v4 on v3

--- a/solution.py
+++ b/solution.py
@@ -68,29 +68,42 @@
     )(routed_slots.reshape(1, cap), tokens)
 
 
-def place(routed_slots, combine, pieces, tokens_here):
+def place(routed_slots, combine, pieces, tokens_here, run, before=None):
     cap = routed_slots.shape[0]
     width = pieces[0][0].shape[1] // 2
 
     def kernel(slots_ref, combine_ref, *refs):
-        out_ref = refs[-1]
-        order = shard_order()
+        out_ref, rows_ref, sems = refs[-3:]
+        shards = shard_order()[4 * run : 4 * run + 4]
         ids = lax.broadcasted_iota(jnp.int32, (tokens_here, cap), 0)
         put = (ids == slots_ref[...]).astype(BF16)
-        for k in range(4):
-            total = refs[2 * k][...].astype(F32) + refs[2 * k + 1][...].astype(F32)
+        copies = []
+        for k in range(2):
+            total = refs[2 * k][...] + refs[2 * k + 1][...].astype(F32)
             value = (combine_ref[...] * total).astype(BF16)
             rows = jnp.dot(put, value, preferred_element_type=F32).astype(BF16)
             for i in range(2):
-                start = pl.multiple_of(order[2 * k + i] * width, 128)
-                out_ref[:, pl.ds(start, width)] = rows[:, i * width : (i + 1) * width]
+                j = 2 * k + i
+                rows_ref[j] = rows[:, i * width : (i + 1) * width]
+                start = pl.multiple_of(shards[j] * width, 128)
+                copies.append(pltpu.make_async_copy(rows_ref.at[j], out_ref.at[:, pl.ds(start, width)], sems.at[j]))
+                copies[j].start()
+        for copy in copies:
+            copy.wait()
 
     flat = [v for pair in pieces for v in pair]
+    in_specs = [pl.BlockSpec(memory_space=pltpu.VMEM)] * (2 + len(flat))
+    aliases = {}
+    if before is not None:
+        aliases = {len(in_specs): 0}
+        in_specs, flat = in_specs + [pl.BlockSpec(memory_space=pl.ANY)], flat + [before]
     return pl.pallas_call(
         kernel,
-        in_specs=[pl.BlockSpec(memory_space=pltpu.VMEM)] * (2 + len(flat)),
-        out_specs=pl.BlockSpec(memory_space=pltpu.VMEM),
+        in_specs=in_specs,
+        out_specs=pl.BlockSpec(memory_space=pl.ANY),
         out_shape=jax.ShapeDtypeStruct((tokens_here, 8 * width), BF16),
+        input_output_aliases=aliases,
+        scratch_shapes=[pltpu.VMEM((4, tokens_here, width), BF16), pltpu.SemaphoreType.DMA((4,))],
         compiler_params=pltpu.CompilerParams(vmem_limit_bytes=16 * 2**20),
         name="place",
     )(routed_slots.reshape(1, cap), combine.reshape(cap, 1), *flat)
@@ -118,11 +131,11 @@
     group = 4 * cap
     p, q = P_OFF, Q_OFF
 
+    w_0 = jnp.concatenate([gate_weight, up_weight], axis=1)
+    near_w = stack(w_0, exchange(w_0, "z", p))
     own_a, own_b = pack(routed_slots, tokens)
     a_1 = stack(own_a, exchange(own_a, "in", p))
     b_1 = stack(own_b, exchange(own_b, "in", q))
-    w_0 = jnp.concatenate([gate_weight, up_weight], axis=1)
-    near_w = stack(w_0, exchange(w_0, "z", p))
     a_2, b_2 = exchange(a_1, "in", q), exchange(b_1, "in", p)
     a0 = stack(a_1, a_2)
     b0 = stack(own_b, b_2[:cap], b_1[cap:], b_2[cap:])
@@ -162,7 +175,8 @@
             got = exchange(stack(one, block(3)).astype(BF16), "in", off).astype(F32)
             last = exchange((two + got[cap:]).astype(BF16), "in", 4 - off)
             pieces.append((block(0) + got[:cap], last))
-    return place(routed_slots, combine_weight, pieces, tokens.shape[0])
+    mixed = place(routed_slots, combine_weight, pieces[2:], tokens.shape[0], 1)
+    return place(routed_slots, combine_weight, pieces[:2], tokens.shape[0], 0, mixed)
 
 
 def solution(mesh):

time: 172 us -> 172 us (level)
  transfers between devices with their start and end apart: 32 -> 32, of which waited for: 15 -> 15; matrix products, arithmetic and copies ran while one was open for 14% -> 14% of each run, Pallas kernels for 0% -> 1%
where the time goes in v4:
time: 172 us; the launch traced here: 171 us
  waiting for transfers between devices  94.2 us (55%)
  starting transfers between devices  47 us (27%)
  matrix products  19.9 us (12%)
  local copies, waits for them, and re-layouts  3.86 us (2%)
  other arithmetic  2.89 us (2%)
  Pallas kernels  2.81 us (2%)
    ppermute x28, waiting for transfers between devices, exchange(): return lax.ppermute(value, BOTH, PAIRS[kind, off])  94.2 us
    ppermute x28, starting transfers between devices, exchange(): return lax.ppermute(value, BOTH, PAIRS[kind, off])  46.4 us
    dot_general x16, matrix products, dot(): return jnp.dot(a, b, preferred_element_type=F32)  19.9 us
  transfers between devices with their start and end apart: 32, of which 15 were waited for; matrix products, arithmetic and copies ran while one was open for 14% of the time, Pallas kernels for 1%

profile of v4, /device:TPU:0, one launch (start us, length us, event | category | flops | bytes accessed | tf_op | source)
XLA Modules:
  0.0 171.5 jit_solution(18384882228401491327)
XLA Ops:
  0.0 1.4 copy-done
  1.4 0.7 copy-done.1
  2.1 0.4 pack.1
  2.5 1.7 collective-permute-start
  4.4 2.0 %collective-permute-start.8 = (bf16[768,1024]{1,0:T(8,128)(2,1)S(1)}, bf16[768,1024]{1,0:T(8,128)(2,1)S(1)}, u32[]{:S(2)}, u32[]{:S(2)}) collective-permute-start(bf16[768,1024]{1,0:T(8,128)(2,1)S(1)} %constant_dynamic-update-slice_fusion.9), channel_id=1, source_target_pairs={{0,32},{1,33},{2,34},{3,35},{4,36},{5,37},{6,38},{7,39},{8,40},{9,... | collective-permute-start | bytes 4718600 | tf_op jit(solution)/shard_map/ppermute | solution.py:31
  6.4 2.1 %collective-permute-start.4 = (bf16[56,3072]{1,0:T(8,128)(2,1)S(1)}, bf16[56,3072]{1,0:T(8,128)(2,1)S(1)}, u32[]{:S(2)}, u32[]{:S(2)}) collective-permute-start(bf16[56,3072]{1,0:T(8,128)(2,1)S(1)} %get-tuple-element.12), channel_id=1, source_target_pairs={{0,3},{1,2},{2,1},{3,0},{4,7},{5,6},{6,5},{7,4},{8,11},{9,10},{10,... | collective-permute-start | bytes 1032200 | tf_op jit(solution)/shard_map/ppermute | solution.py:31
  8.7 1.2 collective-permute-done
  9.9 2.9 %collective-permute-start.1 = (bf16[112,3072]{1,0:T(8,128)(2,1)S(1)}, bf16[112,3072]{1,0:T(8,128)(2,1)S(1)}, u32[]{:S(2)}, u32[]{:S(2)}) collective-permute-start(bf16[112,3072]{1,0:T(8,128)(2,1)S(1)} %pad_maximum_fusion.3), channel_id=1, source_target_pairs={{0,3},{1,2},{2,1},{3,0},{4,7},{5,6},{6,5},{7,4},{8,11},{9,10},{10,... | collective-permute-start | bytes 2064392 | tf_op jit(solution)/shard_map/ppermute | solution.py:31
  12.8 2.1 %collective-permute-done.4 = bf16[56,3072]{1,0:T(8,128)(2,1)S(1)} collective-permute-done((bf16[56,3072]{1,0:T(8,128)(2,1)S(1)}, bf16[56,3072]{1,0:T(8,128)(2,1)S(1)}, u32[]{:S(2)}, u32[]{:S(2)}) %collective-permute-start.4) | collective-permute-done | bytes 344096 | tf_op jit(solution)/shard_map/ppermute | solution.py:31
  15.0 7.2 %collective-permute-done.1 = bf16[112,3072]{1,0:T(8,128)(2,1)S(1)} collective-permute-done((bf16[112,3072]{1,0:T(8,128)(2,1)S(1)}, bf16[112,3072]{1,0:T(8,128)(2,1)S(1)}, u32[]{:S(2)}, u32[]{:S(2)}) %collective-permute-start.1) | collective-permute-done | bytes 688160 | tf_op jit(solution)/shard_map/ppermute | solution.py:31
  22.3 1.7 collective-permute-start.2
  24.0 0.9 collective-permute-done.8
  24.9 0.3 pad_maximum_fusion
  25.2 4.1 %collective-permute-start.10 = (bf16[1536,1024]{1,0:T(8,128)(2,1)S(1)}, bf16[1536,1024]{1,0:T(8,128)(2,1)S(1)}, u32[]{:S(2)}, u32[]{:S(2)}) collective-permute-start(bf16[1536,1024]{1,0:T(8,128)(2,1)S(1)} %pad_maximum_fusion), channel_id=1, source_target_pairs={{0,96},{1,97},{2,98},{3,99},{4,100},{5,101},{6,102},{7,103},{8,104... | collective-permute-start | bytes 9437192 | tf_op jit(solution)/shard_map/ppermute | solution.py:31
  29.6 3.1 %collective-permute-start.6 = (bf16[224,3072]{1,0:T(8,128)(2,1)S(1)}, bf16[224,3072]{1,0:T(8,128)(2,1)S(1)}, u32[]{:S(2)}, u32[]{:S(2)}) collective-permute-start(bf16[224,3072]{1,0:T(8,128)(2,1)S(1)} %pad_maximum_fusion.2), channel_id=1, source_target_pairs={{0,12},{1,13},{2,14},{3,15},{4,8},{5,9},{6,10},{7,11},{8,4},{9,5},... | collective-permute-start | bytes 4128776 | tf_op jit(solution)/shard_map/ppermute | solution.py:31
  32.9 16.3 %collective-permute-done.6 = bf16[224,3072]{1,0:T(8,128)(2,1)S(1)} collective-permute-done((bf16[224,3072]{1,0:T(8,128)(2,1)S(1)}, bf16[224,3072]{1,0:T(8,128)(2,1)S(1)}, u32[]{:S(2)}, u32[]{:S(2)}) %collective-permute-start.6) | collective-permute-done | bytes 1376288 | tf_op jit(solution)/shard_map/ppermute | solution.py:31
  49.2 0.4 collective-permute-start.7
  49.8 2.8 %collective-permute-start.3 = (bf16[448,3072]{1,0:T(8,128)(2,1)S(1)}, bf16[448,3072]{1,0:T(8,128)(2,1)S(1)}, u32[]{:S(2)}, u32[]{:S(2)}) collective-permute-start(bf16[448,3072]{1,0:T(8,128)(2,1)S(1)} %constant_dynamic-update-slice_fusion), channel_id=1, source_target_pairs={{0,12},{1,13},{2,14},{3,15},{4,8},{5,9},{6,10},{7,11},{8,4},{9,5},... | collective-permute-start | bytes 8257544 | tf_op jit(solution)/shard_map/ppermute | solution.py:31
  52.7 1.2 collective-permute-start.22
  53.8 14.2 %collective-permute-done.10 = bf16[1536,1024]{1,0:T(8,128)(2,1)S(1)} collective-permute-done((bf16[1536,1024]{1,0:T(8,128)(2,1)S(1)}, bf16[1536,1024]{1,0:T(8,128)(2,1)S(1)}, u32[]{:S(2)}, u32[]{:S(2)}) %collective-permute-start.10) | collective-permute-done | bytes 3145760 | tf_op jit(solution)/shard_map/ppermute | solution.py:31
  68.0 1.6 fusion.1
  69.6 15.2 %collective-permute-done.22 = bf16[512,1536]{1,0:T(8,128)(2,1)S(1)} collective-permute-done((bf16[512,1536]{1,0:T(8,128)(2,1)S(1)}, bf16[512,1536]{1,0:T(8,128)(2,1)S(1)}, u32[]{:S(2)}, u32[]{:S(2)}) %collective-permute-start.22) | collective-permute-done | bytes 1572896 | tf_op jit(solution)/shard_map/ppermute | solution.py:31
  84.9 0.5 collective-permute-start.27
  85.4 1.6 fusion.3
  87.0 1.6 convolution_add_fusion.6
  88.6 1.6 fusion.6
  90.2 1.6 fusion.10
  91.8 1.6 convolution_add_fusion.4
  93.5 1.6 convolution_add_fusion.5
  95.1 0.4 fusion.24
  95.5 1.6 maximum_add_fusion.1
  97.5 0.3 maximum_add_fusion
  98.1 0.9 convolution_convert_fusion
  99.0 1.1 collective-permute-start.28
  100.1 0.9 convolution_convert_fusion.1
  101.0 2.5 %collective-permute-start.23 = (bf16[448,1536]{1,0:T(8,128)(2,1)S(1)}, bf16[448,1536]{1,0:T(8,128)(2,1)S(1)}, u32[]{:S(2)}, u32[]{:S(2)}) collective-permute-start(bf16[448,1536]{1,0:T(8,128)(2,1)S(1)} %convolution_convert_fusion.1), channel_id=1, source_target_pairs={{0,12},{1,13},{2,14},{3,15},{4,8},{5,9},{6,10},{7,11},{8,4},{9,5},... | collective-permute-start | bytes 4128776 | tf_op jit(solution)/shard_map/ppermute | solution.py:31
  103.5 0.9 convolution_convert_fusion.2
  104.4 0.7 collective-permute-start.18
  105.1 0.9 convolution_convert_fusion.3
  106.0 0.9 collective-permute-start.13
  106.9 10.5 %collective-permute-done.28 = bf16[448,1536]{1,0:T(8,128)(2,1)S(1)} collective-permute-done((bf16[448,1536]{1,0:T(8,128)(2,1)S(1)}, bf16[448,1536]{1,0:T(8,128)(2,1)S(1)}, u32[]{:S(2)}, u32[]{:S(2)}) %collective-permute-start.28) | collective-permute-done | bytes 1376288 | tf_op jit(solution)/shard_map/ppermute | solution.py:31
  117.4 0.9 convolution_add_fusion
  118.4 2.5 %collective-permute-start.29 = (bf16[224,1536]{1,0:T(8,128)(2,1)S(1)}, bf16[224,1536]{1,0:T(8,128)(2,1)S(1)}, u32[]{:S(2)}, u32[]{:S(2)}) collective-permute-start(bf16[224,1536]{1,0:T(8,128)(2,1)S(1)} %slice.320), channel_id=1, source_target_pairs={{0,12},{1,13},{2,14},{3,15},{4,8},{5,9},{6,10},{7,11},{8,4},{9,5},... | collective-permute-start | bytes 2064392 | tf_op jit(solution)/shard_map/ppermute | solution.py:31
  120.9 0.9 convolution_add_fusion.1
  121.9 0.5 collective-permute-start.24
  122.4 9.8 %collective-permute-done.18 = bf16[448,1536]{1,0:T(8,128)(2,1)S(1)} collective-permute-done((bf16[448,1536]{1,0:T(8,128)(2,1)S(1)}, bf16[448,1536]{1,0:T(8,128)(2,1)S(1)}, u32[]{:S(2)}, u32[]{:S(2)}) %collective-permute-start.18) | collective-permute-done | bytes 1376288 | tf_op jit(solution)/shard_map/ppermute | solution.py:31
  132.2 0.9 convolution_add_fusion.2
  133.1 2.5 %collective-permute-start.19 = (bf16[224,1536]{1,0:T(8,128)(2,1)S(1)}, bf16[224,1536]{1,0:T(8,128)(2,1)S(1)}, u32[]{:S(2)}, u32[]{:S(2)}) collective-permute-start(bf16[224,1536]{1,0:T(8,128)(2,1)S(1)} %slice.322), channel_id=1, source_target_pairs={{0,12},{1,13},{2,14},{3,15},{4,8},{5,9},{6,10},{7,11},{8,4},{9,5},... | collective-permute-start | bytes 2064392 | tf_op jit(solution)/shard_map/ppermute | solution.py:31
  135.7 0.9 convolution_add_fusion.3
  136.6 0.5 collective-permute-start.14
  137.1 5.6 %collective-permute-done.29 = bf16[224,1536]{1,0:T(8,128)(2,1)S(1)} collective-permute-done((bf16[224,1536]{1,0:T(8,128)(2,1)S(1)}, bf16[224,1536]{1,0:T(8,128)(2,1)S(1)}, u32[]{:S(2)}, u32[]{:S(2)}) %collective-permute-start.29) | collective-permute-done | bytes 688160 | tf_op jit(solution)/shard_map/ppermute | solution.py:31
  143.0 1.6 collective-permute-start.30
  144.8 2.2 %collective-permute-start.25 = (bf16[112,1536]{1,0:T(8,128)(2,1)S(1)}, bf16[112,1536]{1,0:T(8,128)(2,1)S(1)}, u32[]{:S(2)}, u32[]{:S(2)}) collective-permute-start(bf16[112,1536]{1,0:T(8,128)(2,1)S(1)} %concatenate.77), channel_id=1, source_target_pairs={{0,3},{1,2},{2,1},{3,0},{4,7},{5,6},{6,5},{7,4},{8,11},{9,10},{10,... | collective-permute-start | bytes 1032200 | tf_op jit(solution)/shard_map/ppermute | solution.py:31
  147.0 6.2 %collective-permute-done.19 = bf16[224,1536]{1,0:T(8,128)(2,1)S(1)} collective-permute-done((bf16[224,1536]{1,0:T(8,128)(2,1)S(1)}, bf16[224,1536]{1,0:T(8,128)(2,1)S(1)}, u32[]{:S(2)}, u32[]{:S(2)}) %collective-permute-start.19) | collective-permute-done | bytes 688160 | tf_op jit(solution)/shard_map/ppermute | solution.py:31
  153.4 2.2 %collective-permute-start.20 = (bf16[112,1536]{1,0:T(8,128)(2,1)S(1)}, bf16[112,1536]{1,0:T(8,128)(2,1)S(1)}, u32[]{:S(2)}, u32[]{:S(2)}) collective-permute-start(bf16[112,1536]{1,0:T(8,128)(2,1)S(1)} %pad_maximum_fusion.7), channel_id=1, source_target_pairs={{0,1},{1,0},{2,3},{3,2},{4,5},{5,4},{6,7},{7,6},{8,9},{9,8},{10,11... | collective-permute-start | bytes 1032200 | tf_op jit(solution)/shard_map/ppermute | solution.py:31
  155.8 2.2 %collective-permute-start.15 = (bf16[112,1536]{1,0:T(8,128)(2,1)S(1)}, bf16[112,1536]{1,0:T(8,128)(2,1)S(1)}, u32[]{:S(2)}, u32[]{:S(2)}) collective-permute-start(bf16[112,1536]{1,0:T(8,128)(2,1)S(1)} %concatenate.78), channel_id=1, source_target_pairs={{0,3},{1,2},{2,1},{3,0},{4,7},{5,6},{6,5},{7,4},{8,11},{9,10},{10,... | collective-permute-start | bytes 1032200 | tf_op jit(solution)/shard_map/ppermute | solution.py:31
  158.2 1.2 collective-permute-start.31
  159.7 1.2 collective-permute-done.20
  161.1 3.4 %collective-permute-start.21 = (bf16[56,1536]{1,0:T(8,128)(2,1)S(1)}, bf16[56,1536]{1,0:T(8,128)(2,1)S(1)}, u32[]{:S(2)}, u32[]{:S(2)}) collective-permute-start(bf16[56,1536]{1,0:T(8,128)(2,1)S(1)} %get-tuple-element.25), channel_id=1, source_target_pairs={{0,3},{1,2},{2,1},{3,0},{4,7},{5,6},{6,5},{7,4},{8,11},{9,10},{10,... | collective-permute-start | bytes 516104 | tf_op jit(solution)/shard_map/ppermute | solution.py:31
  165.0 1.2 collective-permute-done.31.refs_3_
  166.2 1.2 place.2.refs_4_
  167.4 0.6 collective-permute-done.21.refs_3_
  168.1 2.0 %collective-permute-done.16.refs_1_ = bf16[56,1536]{1,0:T(8,128)(2,1)S(1)} collective-permute-done((bf16[56,1536]{1,0:T(8,128)(2,1)S(1)}, bf16[56,1536]{1,0:T(8,128)(2,1)S(1)}, u32[]{:S(2)}, u32[]{:S(2)}) %collective-permute-start.16) | collective-permute-done | bytes 172064 | tf_op jit(solution)/shard_map/ppermute | solution.py:31
  170.1 1.2 place.3
  (80 shorter events, 4.3 us)
Async XLA Ops:
  0.0 1.4 copy-start
  1.4 0.7 copy-start.1
  2.1 2.1 %copy-start.3 = (bf16[768,512]{1,0:T(8,128)(2,1)S(1)}, bf16[768,512]{1,0:T(8,128)(2,1)}, u32[]{:S(2)}) copy-start(bf16[768,512]{1,0:T(8,128)(2,1)} %param.9) | copy-start | bytes 2359300
  2.1 2.2 %copy-start.4 = (bf16[768,512]{1,0:T(8,128)(2,1)S(1)}, bf16[768,512]{1,0:T(8,128)(2,1)}, u32[]{:S(2)}) copy-start(bf16[768,512]{1,0:T(8,128)(2,1)} %param.10) | copy-start | bytes 2359300
  2.5 6.0 %copy-start.5 = (bf16[512,768]{1,0:T(8,128)(2,1)S(1)}, bf16[512,768]{1,0:T(8,128)(2,1)}, u32[]{:S(2)}) copy-start(bf16[512,768]{1,0:T(8,128)(2,1)} %param.11) | copy-start | bytes 2359300
  2.5 7.3 %collective-permute-start = (bf16[56,3072]{1,0:T(8,128)(2,1)S(1)}, bf16[56,3072]{1,0:T(8,128)(2,1)S(1)}, u32[]{:S(2)}, u32[]{:S(2)}) collective-permute-start(bf16[56,3072]{1,0:T(8,128)(2,1)S(1)} %get-tuple-element.11), channel_id=1, source_target_pairs={{0,1},{1,0},{2,3},{3,2},{4,5},{5,4},{6,7},{7,6},{8,9},{9,8},{10,11... | collective-permute-start | bytes 1032200 | tf_op jit(solution)/shard_map/ppermute | solution.py:31
  4.4 20.5 %collective-permute-start.8 = (bf16[768,1024]{1,0:T(8,128)(2,1)S(1)}, bf16[768,1024]{1,0:T(8,128)(2,1)S(1)}, u32[]{:S(2)}, u32[]{:S(2)}) collective-permute-start(bf16[768,1024]{1,0:T(8,128)(2,1)S(1)} %constant_dynamic-update-slice_fusion.9), channel_id=1, source_target_pairs={{0,32},{1,33},{2,34},{3,35},{4,36},{5,37},{6,38},{7,39},{8,40},{9,... | collective-permute-start | bytes 4718600 | tf_op jit(solution)/shard_map/ppermute | solution.py:31
  6.4 8.5 %collective-permute-start.4 = (bf16[56,3072]{1,0:T(8,128)(2,1)S(1)}, bf16[56,3072]{1,0:T(8,128)(2,1)S(1)}, u32[]{:S(2)}, u32[]{:S(2)}) collective-permute-start(bf16[56,3072]{1,0:T(8,128)(2,1)S(1)} %get-tuple-element.12), channel_id=1, source_target_pairs={{0,3},{1,2},{2,1},{3,0},{4,7},{5,6},{6,5},{7,4},{8,11},{9,10},{10,... | collective-permute-start | bytes 1032200 | tf_op jit(solution)/shard_map/ppermute | solution.py:31
  8.5 44.1 %collective-permute-start.12 = (bf16[512,768]{1,0:T(8,128)(2,1)S(1)}, bf16[512,768]{1,0:T(8,128)(2,1)S(1)}, u32[]{:S(2)}, u32[]{:S(2)}) collective-permute-start(bf16[512,768]{1,0:T(8,128)(2,1)S(1)} %copy-done.5), channel_id=1, source_target_pairs={{0,32},{1,33},{2,34},{3,35},{4,36},{5,37},{6,38},{7,39},{8,40},{9,... | collective-permute-start | bytes 2359304 | tf_op jit(solution)/shard_map/ppermute | solution.py:31
  9.9 12.3 %collective-permute-start.1 = (bf16[112,3072]{1,0:T(8,128)(2,1)S(1)}, bf16[112,3072]{1,0:T(8,128)(2,1)S(1)}, u32[]{:S(2)}, u32[]{:S(2)}) collective-permute-start(bf16[112,3072]{1,0:T(8,128)(2,1)S(1)} %pad_maximum_fusion.3), channel_id=1, source_target_pairs={{0,3},{1,2},{2,1},{3,0},{4,7},{5,6},{6,5},{7,4},{8,11},{9,10},{10,... | collective-permute-start | bytes 2064392 | tf_op jit(solution)/shard_map/ppermute | solution.py:31
  14.9 14.4 %collective-permute-start.5 = (bf16[112,3072]{1,0:T(8,128)(2,1)S(1)}, bf16[112,3072]{1,0:T(8,128)(2,1)S(1)}, u32[]{:S(2)}, u32[]{:S(2)}) collective-permute-start(bf16[112,3072]{1,0:T(8,128)(2,1)S(1)} %pad_maximum_fusion.4), channel_id=1, source_target_pairs={{0,1},{1,0},{2,3},{3,2},{4,5},{5,4},{6,7},{7,6},{8,9},{9,8},{10,11... | collective-permute-start | bytes 2064392 | tf_op jit(solution)/shard_map/ppermute | solution.py:31
  22.3 27.4 %collective-permute-start.2 = (bf16[224,3072]{1,0:T(8,128)(2,1)S(1)}, bf16[224,3072]{1,0:T(8,128)(2,1)S(1)}, u32[]{:S(2)}, u32[]{:S(2)}) collective-permute-start(bf16[224,3072]{1,0:T(8,128)(2,1)S(1)} %pad_maximum_fusion.1), channel_id=1, source_target_pairs={{0,4},{1,5},{2,6},{3,7},{4,0},{5,1},{6,2},{7,3},{8,12},{9,13},{10,... | collective-permute-start | bytes 4128776 | tf_op jit(solution)/shard_map/ppermute | solution.py:31
  25.2 42.8 %collective-permute-start.10 = (bf16[1536,1024]{1,0:T(8,128)(2,1)S(1)}, bf16[1536,1024]{1,0:T(8,128)(2,1)S(1)}, u32[]{:S(2)}, u32[]{:S(2)}) collective-permute-start(bf16[1536,1024]{1,0:T(8,128)(2,1)S(1)} %pad_maximum_fusion), channel_id=1, source_target_pairs={{0,96},{1,97},{2,98},{3,99},{4,100},{5,101},{6,102},{7,103},{8,104... | collective-permute-start | bytes 9437192 | tf_op jit(solution)/shard_map/ppermute | solution.py:31
  29.6 19.6 %collective-permute-start.6 = (bf16[224,3072]{1,0:T(8,128)(2,1)S(1)}, bf16[224,3072]{1,0:T(8,128)(2,1)S(1)}, u32[]{:S(2)}, u32[]{:S(2)}) collective-permute-start(bf16[224,3072]{1,0:T(8,128)(2,1)S(1)} %pad_maximum_fusion.2), channel_id=1, source_target_pairs={{0,12},{1,13},{2,14},{3,15},{4,8},{5,9},{6,10},{7,11},{8,4},{9,5},... | collective-permute-start | bytes 4128776 | tf_op jit(solution)/shard_map/ppermute | solution.py:31
  32.7 52.1 %collective-permute-start.9 = (bf16[1536,1024]{1,0:T(8,128)(2,1)S(1)}, bf16[1536,1024]{1,0:T(8,128)(2,1)S(1)}, u32[]{:S(2)}, u32[]{:S(2)}) collective-permute-start(bf16[1536,1024]{1,0:T(8,128)(2,1)S(1)} %pad_maximum_fusion), channel_id=1, source_target_pairs={{0,16},{1,17},{2,18},{3,19},{4,20},{5,21},{6,22},{7,23},{8,24},{9,... | collective-permute-start | bytes 9437192 | tf_op jit(solution)/shard_map/ppermute | solution.py:35
  49.2 39.3 %collective-permute-start.7 = (bf16[448,3072]{1,0:T(8,128)(2,1)S(1)}, bf16[448,3072]{1,0:T(8,128)(2,1)S(1)}, u32[]{:S(2)}, u32[]{:S(2)}) collective-permute-start(bf16[448,3072]{1,0:T(8,128)(2,1)S(1)} %constant_dynamic-update-slice_fusion.4), channel_id=1, source_target_pairs={{0,4},{1,5},{2,6},{3,7},{4,0},{5,1},{6,2},{7,3},{8,12},{9,13},{10,... | collective-permute-start | bytes 8257544 | tf_op jit(solution)/shard_map/ppermute | solution.py:31
  49.8 38.8 %collective-permute-start.3 = (bf16[448,3072]{1,0:T(8,128)(2,1)S(1)}, bf16[448,3072]{1,0:T(8,128)(2,1)S(1)}, u32[]{:S(2)}, u32[]{:S(2)}) collective-permute-start(bf16[448,3072]{1,0:T(8,128)(2,1)S(1)} %constant_dynamic-update-slice_fusion), channel_id=1, source_target_pairs={{0,12},{1,13},{2,14},{3,15},{4,8},{5,9},{6,10},{7,11},{8,4},{9,5},... | collective-permute-start | bytes 8257544 | tf_op jit(solution)/shard_map/ppermute | solution.py:31
  52.7 32.2 %collective-permute-start.22 = (bf16[512,1536]{1,0:T(8,128)(2,1)S(1)}, bf16[512,1536]{1,0:T(8,128)(2,1)S(1)}, u32[]{:S(2)}, u32[]{:S(2)}) collective-permute-start(bf16[512,1536]{1,0:T(8,128)(2,1)S(1)} %constant_dynamic-update-slice_fusion.11), channel_id=1, source_target_pairs={{0,96},{1,97},{2,98},{3,99},{4,100},{5,101},{6,102},{7,103},{8,104... | collective-permute-start | bytes 4718600 | tf_op jit(solution)/shard_map/ppermute | solution.py:31
  68.0 23.8 %collective-permute-start.11 = (bf16[1536,1024]{1,0:T(8,128)(2,1)S(1)}, bf16[1536,1024]{1,0:T(8,128)(2,1)S(1)}, u32[]{:S(2)}, u32[]{:S(2)}) collective-permute-start(bf16[1536,1024]{1,0:T(8,128)(2,1)S(1)} %collective-permute-done.10), channel_id=1, source_target_pairs={{0,16},{1,17},{2,18},{3,19},{4,20},{5,21},{6,22},{7,23},{8,24},{9,... | collective-permute-start | bytes 9437192 | tf_op jit(solution)/shard_map/ppermute | solution.py:35
  84.8 18.7 %collective-permute-start.17 = (bf16[512,1536]{1,0:T(8,128)(2,1)S(1)}, bf16[512,1536]{1,0:T(8,128)(2,1)S(1)}, u32[]{:S(2)}, u32[]{:S(2)}) collective-permute-start(bf16[512,1536]{1,0:T(8,128)(2,1)S(1)} %constant_dynamic-update-slice_fusion.11), channel_id=1, source_target_pairs={{0,16},{1,17},{2,18},{3,19},{4,20},{5,21},{6,22},{7,23},{8,24},{9,... | collective-permute-start | bytes 4718600 | tf_op jit(solution)/shard_map/ppermute | solution.py:35
  84.9 13.3 %collective-permute-start.27 = (bf16[512,1536]{1,0:T(8,128)(2,1)S(1)}, bf16[512,1536]{1,0:T(8,128)(2,1)S(1)}, u32[]{:S(2)}, u32[]{:S(2)}) collective-permute-start(bf16[512,1536]{1,0:T(8,128)(2,1)S(1)} %collective-permute-done.22), channel_id=1, source_target_pairs={{0,16},{1,17},{2,18},{3,19},{4,20},{5,21},{6,22},{7,23},{8,24},{9,... | collective-permute-start | bytes 4718600 | tf_op jit(solution)/shard_map/ppermute | solution.py:35
  99.0 18.4 %collective-permute-start.28 = (bf16[448,1536]{1,0:T(8,128)(2,1)S(1)}, bf16[448,1536]{1,0:T(8,128)(2,1)S(1)}, u32[]{:S(2)}, u32[]{:S(2)}) collective-permute-start(bf16[448,1536]{1,0:T(8,128)(2,1)S(1)} %convolution_convert_fusion), channel_id=1, source_target_pairs={{0,4},{1,5},{2,6},{3,7},{4,0},{5,1},{6,2},{7,3},{8,12},{9,13},{10,... | collective-permute-start | bytes 4128776 | tf_op jit(solution)/shard_map/ppermute | solution.py:31
  101.0 19.9 %collective-permute-start.23 = (bf16[448,1536]{1,0:T(8,128)(2,1)S(1)}, bf16[448,1536]{1,0:T(8,128)(2,1)S(1)}, u32[]{:S(2)}, u32[]{:S(2)}) collective-permute-start(bf16[448,1536]{1,0:T(8,128)(2,1)S(1)} %convolution_convert_fusion.1), channel_id=1, source_target_pairs={{0,12},{1,13},{2,14},{3,15},{4,8},{5,9},{6,10},{7,11},{8,4},{9,5},... | collective-permute-start | bytes 4128776 | tf_op jit(solution)/shard_map/ppermute | solution.py:31
  104.4 27.7 %collective-permute-start.18 = (bf16[448,1536]{1,0:T(8,128)(2,1)S(1)}, bf16[448,1536]{1,0:T(8,128)(2,1)S(1)}, u32[]{:S(2)}, u32[]{:S(2)}) collective-permute-start(bf16[448,1536]{1,0:T(8,128)(2,1)S(1)} %convolution_convert_fusion.2), channel_id=1, source_target_pairs={{0,4},{1,5},{2,6},{3,7},{4,0},{5,1},{6,2},{7,3},{8,12},{9,13},{10,... | collective-permute-start | bytes 4128776 | tf_op jit(solution)/shard_map/ppermute | solution.py:31
  106.0 29.6 %collective-permute-start.13 = (bf16[448,1536]{1,0:T(8,128)(2,1)S(1)}, bf16[448,1536]{1,0:T(8,128)(2,1)S(1)}, u32[]{:S(2)}, u32[]{:S(2)}) collective-permute-start(bf16[448,1536]{1,0:T(8,128)(2,1)S(1)} %convolution_convert_fusion.3), channel_id=1, source_target_pairs={{0,12},{1,13},{2,14},{3,15},{4,8},{5,9},{6,10},{7,11},{8,4},{9,5},... | collective-permute-start | bytes 4128776 | tf_op jit(solution)/shard_map/ppermute | solution.py:31
  118.4 24.3 %collective-permute-start.29 = (bf16[224,1536]{1,0:T(8,128)(2,1)S(1)}, bf16[224,1536]{1,0:T(8,128)(2,1)S(1)}, u32[]{:S(2)}, u32[]{:S(2)}) collective-permute-start(bf16[224,1536]{1,0:T(8,128)(2,1)S(1)} %slice.320), channel_id=1, source_target_pairs={{0,12},{1,13},{2,14},{3,15},{4,8},{5,9},{6,10},{7,11},{8,4},{9,5},... | collective-permute-start | bytes 2064392 | tf_op jit(solution)/shard_map/ppermute | solution.py:31
  121.9 22.7 %collective-permute-start.24 = (bf16[224,1536]{1,0:T(8,128)(2,1)S(1)}, bf16[224,1536]{1,0:T(8,128)(2,1)S(1)}, u32[]{:S(2)}, u32[]{:S(2)}) collective-permute-start(bf16[224,1536]{1,0:T(8,128)(2,1)S(1)} %slice.321), channel_id=1, source_target_pairs={{0,4},{1,5},{2,6},{3,7},{4,0},{5,1},{6,2},{7,3},{8,12},{9,13},{10,... | collective-permute-start | bytes 2064392 | tf_op jit(solution)/shard_map/ppermute | solution.py:31
  133.1 20.0 %collective-permute-start.19 = (bf16[224,1536]{1,0:T(8,128)(2,1)S(1)}, bf16[224,1536]{1,0:T(8,128)(2,1)S(1)}, u32[]{:S(2)}, u32[]{:S(2)}) collective-permute-start(bf16[224,1536]{1,0:T(8,128)(2,1)S(1)} %slice.322), channel_id=1, source_target_pairs={{0,12},{1,13},{2,14},{3,15},{4,8},{5,9},{6,10},{7,11},{8,4},{9,5},... | collective-permute-start | bytes 2064392 | tf_op jit(solution)/shard_map/ppermute | solution.py:31
  136.6 19.0 %collective-permute-start.14 = (bf16[224,1536]{1,0:T(8,128)(2,1)S(1)}, bf16[224,1536]{1,0:T(8,128)(2,1)S(1)}, u32[]{:S(2)}, u32[]{:S(2)}) collective-permute-start(bf16[224,1536]{1,0:T(8,128)(2,1)S(1)} %slice.323), channel_id=1, source_target_pairs={{0,4},{1,5},{2,6},{3,7},{4,0},{5,1},{6,2},{7,3},{8,12},{9,13},{10,... | collective-permute-start | bytes 2064392 | tf_op jit(solution)/shard_map/ppermute | solution.py:31
  143.0 15.0 %collective-permute-start.30 = (bf16[112,1536]{1,0:T(8,128)(2,1)S(1)}, bf16[112,1536]{1,0:T(8,128)(2,1)S(1)}, u32[]{:S(2)}, u32[]{:S(2)}) collective-permute-start(bf16[112,1536]{1,0:T(8,128)(2,1)S(1)} %pad_maximum_fusion.8), channel_id=1, source_target_pairs={{0,1},{1,0},{2,3},{3,2},{4,5},{5,4},{6,7},{7,6},{8,9},{9,8},{10,11... | collective-permute-start | bytes 1032200 | tf_op jit(solution)/shard_map/ppermute | solution.py:31
  144.8 14.6 %collective-permute-start.25 = (bf16[112,1536]{1,0:T(8,128)(2,1)S(1)}, bf16[112,1536]{1,0:T(8,128)(2,1)S(1)}, u32[]{:S(2)}, u32[]{:S(2)}) collective-permute-start(bf16[112,1536]{1,0:T(8,128)(2,1)S(1)} %concatenate.77), channel_id=1, source_target_pairs={{0,3},{1,2},{2,1},{3,0},{4,7},{5,6},{6,5},{7,4},{8,11},{9,10},{10,... | collective-permute-start | bytes 1032200 | tf_op jit(solution)/shard_map/ppermute | solution.py:31
  153.4 7.4 %collective-permute-start.20 = (bf16[112,1536]{1,0:T(8,128)(2,1)S(1)}, bf16[112,1536]{1,0:T(8,128)(2,1)S(1)}, u32[]{:S(2)}, u32[]{:S(2)}) collective-permute-start(bf16[112,1536]{1,0:T(8,128)(2,1)S(1)} %pad_maximum_fusion.7), channel_id=1, source_target_pairs={{0,1},{1,0},{2,3},{3,2},{4,5},{5,4},{6,7},{7,6},{8,9},{9,8},{10,11... | collective-permute-start | bytes 1032200 | tf_op jit(solution)/shard_map/ppermute | solution.py:31
  155.8 8.6 %collective-permute-start.15 = (bf16[112,1536]{1,0:T(8,128)(2,1)S(1)}, bf16[112,1536]{1,0:T(8,128)(2,1)S(1)}, u32[]{:S(2)}, u32[]{:S(2)}) collective-permute-start(bf16[112,1536]{1,0:T(8,128)(2,1)S(1)} %concatenate.78), channel_id=1, source_target_pairs={{0,3},{1,2},{2,1},{3,0},{4,7},{5,6},{6,5},{7,4},{8,11},{9,10},{10,... | collective-permute-start | bytes 1032200 | tf_op jit(solution)/shard_map/ppermute | solution.py:31
  158.2 8.0 %collective-permute-start.31 = (bf16[56,1536]{1,0:T(8,128)(2,1)S(1)}, bf16[56,1536]{1,0:T(8,128)(2,1)S(1)}, u32[]{:S(2)}, u32[]{:S(2)}) collective-permute-start(bf16[56,1536]{1,0:T(8,128)(2,1)S(1)} %get-tuple-element.21), channel_id=1, source_target_pairs={{0,3},{1,2},{2,1},{3,0},{4,7},{5,6},{6,5},{7,4},{8,11},{9,10},{10,... | collective-permute-start | bytes 516104 | tf_op jit(solution)/shard_map/ppermute | solution.py:31
  159.6 6.6 %collective-permute-start.26 = (bf16[56,1536]{1,0:T(8,128)(2,1)S(1)}, bf16[56,1536]{1,0:T(8,128)(2,1)S(1)}, u32[]{:S(2)}, u32[]{:S(2)}) collective-permute-start(bf16[56,1536]{1,0:T(8,128)(2,1)S(1)} %get-tuple-element.23), channel_id=1, source_target_pairs={{0,1},{1,0},{2,3},{3,2},{4,5},{5,4},{6,7},{7,6},{8,9},{9,8},{10,11... | collective-permute-start | bytes 516104 | tf_op jit(solution)/shard_map/ppermute | solution.py:31
  161.0 3.9 %copy-start.6 = (f32[56]{0:T(128)S(1)}, f32[56]{0:T(128)}, u32[]{:S(2)}) copy-start(f32[56]{0:T(128)} %param.8) | copy-start | bytes 676
  161.0 5.2 %copy-start.2 = (s32[56]{0:T(128)S(1)}, s32[56]{0:T(128)}, u32[]{:S(2)}) copy-start(s32[56]{0:T(128)} %param.7) | copy-start | bytes 676
  161.1 7.0 %collective-permute-start.21 = (bf16[56,1536]{1,0:T(8,128)(2,1)S(1)}, bf16[56,1536]{1,0:T(8,128)(2,1)S(1)}, u32[]{:S(2)}, u32[]{:S(2)}) collective-permute-start(bf16[56,1536]{1,0:T(8,128)(2,1)S(1)} %get-tuple-element.25), channel_id=1, source_target_pairs={{0,3},{1,2},{2,1},{3,0},{4,7},{5,6},{6,5},{7,4},{8,11},{9,10},{10,... | collective-permute-start | bytes 516104 | tf_op jit(solution)/shard_map/ppermute | solution.py:31
  164.6 5.5 %collective-permute-start.16 = (bf16[56,1536]{1,0:T(8,128)(2,1)S(1)}, bf16[56,1536]{1,0:T(8,128)(2,1)S(1)}, u32[]{:S(2)}, u32[]{:S(2)}) collective-permute-start(bf16[56,1536]{1,0:T(8,128)(2,1)S(1)} %get-tuple-element.27), channel_id=1, source_target_pairs={{0,1},{1,0},{2,3},{3,2},{4,5},{5,4},{6,7},{7,6},{8,9},{9,8},{10,11... | collective-permute-start | bytes 516104 | tf_op jit(solution)/shard_map/ppermute | solution.py:31
